TPU v7x, 32 devices: a whole 2x2x4 slice. The times are simulated.
32 devices in a mesh: req: 16 (over z, y, x), head: 2 (over core).
Axes of the slice: x: 2, y: 2, z: 4, core: 2. Of those that a mesh axis runs over, the one named last changes fastest.
Arguments:
- inner_input: bfloat16 [4096, 16384], P('req', 'head'), may hold values from -6 to 6
- projection_input: bfloat16 [4096, 8, 2, 128], P('req', 'head'), may hold values from -6 to 6
- step_before_bias: bfloat16 [4096, 256], P('req', 'head'), may hold values from -2 to 11
- inner_conv_taps: float32 [4, 16384], P(None, 'head'), may hold values from -3 to 3
- projection_conv_taps: float32 [4, 8, 2, 128], P(None, 'head'), may hold values from -3 to 3
- step_bias: float32 [256], P('head'), may hold values from -4.5 to -3.5
- head_decay_rate: float32 [256], P('head'), may hold values from 0.1 to 3
- head_skip_gain: float32 [256], P('head'), may hold values from 0.5 to 1.5
- group_norm_gain: float32 [16384], P('head'), may hold values from 0.5 to 1.5
- tenant: int32 [16], P('req'), may hold values from 0 to 15
- tenant_adapter_row: int32 [16], replicated, may hold values from 0 to 15, each once
- cache_holder_index: int32 [16], P('req'), may hold values from 0 to 15, as said below
- cache_slot_index: int32 [16], P('req'), may hold values from 0 to 1
- adapter_down_panels: bfloat16 [16, 16384, 64], P('req', 'head'), may hold values from -0.046875 to 0.046875
- adapter_up_panels: bfloat16 [16, 64, 8192], P('req', None, 'head'), may hold values from -0.75 to 0.75
- cached_ssm_states: bfloat16 [32, 256, 64, 128], P('req', 'head'), may hold values from -2.5 to 2.5
- inner_conv_cache: bfloat16 [32, 3, 16384], P('req', None, 'head'), may hold values from -6 to 6
- projection_conv_cache: bfloat16 [32, 3, 8, 2, 128], P('req', None, 'head'), may hold values from -6 to 6
Outputs:
- normed_output: bfloat16 [4096, 16384], P('req', 'head')
- adapter_output_term: bfloat16 [4096, 8192], P('req', 'head')
- updated_state: bfloat16 [16, 256, 64, 128], P('req', 'head')
Inputs may be any that keep to these rules, and one draw needn't show every extreme that they name: `tenant_adapter_row`: every row of the adapter tables belongs to exactly one tenant. `cache_holder_index`: no two requests share a cache slot, and each index of req holds the cached states of exactly 1 request.
All inputs are finite; a program needn't handle non-finite values.
Results may differ from a plain program's by a relative error of at most 0.013.
Values may be sent and summed in bfloat16 or wider, within the bound.
A program may use at most 128 MiB of HBM per device.

v0:
```python
import jax
import jax.numpy as jnp
from jax import lax
from jax.sharding import PartitionSpec as P

ADAPTER_SCALE = 2.0
NORM_EPSILON = 1e-05


def causal_conv(cached, current, weight):
    joined = jnp.concatenate([cached, current], axis=1)
    length_value = current.shape[1]
    summed = weight[0] * joined[:, 0:length_value]
    for tap in range(1, weight.shape[0]):
        summed = summed + weight[tap] * joined[:, tap : tap + length_value]
    return jax.nn.silu(summed).astype(jnp.bfloat16)


def per_device(
    inner_input,
    projection_input,
    step_before_bias,
    inner_conv_taps,
    projection_conv_taps,
    step_bias,
    head_decay_rate,
    head_skip_gain,
    group_norm_gain,
    tenant,
    tenant_adapter_row,
    cache_holder_index,
    cache_slot_index,
    adapter_down_panels,
    adapter_up_panels,
    cached_ssm_states,
    inner_conv_cache,
    projection_conv_cache,
):
    per_device_share = tenant.shape[0]
    slots_dev = cached_ssm_states.shape[0]
    hidden_features_on_card = inner_input.shape[1]
    heads_dev = step_before_bias.shape[1]
    groups_dev = projection_input.shape[1]
    state_size = projection_input.shape[3]
    head_size = hidden_features_on_card // heads_dev
    per_group = heads_dev // groups_dev
    reduced_width = adapter_down_panels.shape[2]
    model_per_device = adapter_up_panels.shape[2]
    tap_count = inner_conv_taps.shape[0]
    length_value = inner_input.shape[0] // per_device_share
    tenant_all, owner_all, slot_all = (
        lax.all_gather(tenant, "req", axis=0, tiled=True),
        lax.all_gather(cache_holder_index, "req", axis=0, tiled=True),
        lax.all_gather(cache_slot_index, "req", axis=0, tiled=True),
    )
    customer_identifiers = jnp.arange(tenant_adapter_row.shape[0], dtype=jnp.int32)
    picked_customer_matrix_pair = jnp.sum(
        jnp.where(
            tenant_all[:, None] == customer_identifiers[None, :], tenant_adapter_row[None, :], 0
        ),
        axis=1,
    )
    ssm_flat = cached_ssm_states.reshape(slots_dev, -1)
    convx_flat = inner_conv_cache.reshape(slots_dev, -1)
    convbc_flat = projection_conv_cache.reshape(slots_dev, -1)
    cache_pick = owner_all * slots_dev + slot_all
    dispersion_factor = (
        lax.all_to_all(
            adapter_down_panels.reshape(adapter_down_panels.shape[0], -1),
            "req",
            split_axis=1,
            concat_axis=0,
            tiled=True,
        ),
        lax.all_to_all(
            adapter_up_panels.reshape(adapter_up_panels.shape[0], -1),
            "req",
            split_axis=1,
            concat_axis=0,
            tiled=True,
        ),
        lax.all_to_all(ssm_flat, "req", split_axis=1, concat_axis=0, tiled=True),
        lax.all_to_all(convx_flat, "req", split_axis=1, concat_axis=0, tiled=True),
        lax.all_to_all(convbc_flat, "req", split_axis=1, concat_axis=0, tiled=True),
    )
    picked_left_factor = jnp.take(dispersion_factor[0], picked_customer_matrix_pair, axis=0)
    picked_right_factor = jnp.take(dispersion_factor[1], picked_customer_matrix_pair, axis=0)
    chosen_state = jnp.take(dispersion_factor[2], cache_pick, axis=0)
    chosen_convx = jnp.take(dispersion_factor[3], cache_pick, axis=0)
    chosen_convbc = jnp.take(dispersion_factor[4], cache_pick, axis=0)
    fetched = (
        lax.all_to_all(picked_left_factor, "req", split_axis=0, concat_axis=1, tiled=True),
        lax.all_to_all(picked_right_factor, "req", split_axis=0, concat_axis=1, tiled=True),
        lax.all_to_all(chosen_state, "req", split_axis=0, concat_axis=1, tiled=True),
        lax.all_to_all(chosen_convx, "req", split_axis=0, concat_axis=1, tiled=True),
        lax.all_to_all(chosen_convbc, "req", split_axis=0, concat_axis=1, tiled=True),
    )
    down_panel = fetched[0].reshape(per_device_share, hidden_features_on_card, reduced_width)
    up_panel = fetched[1].reshape(per_device_share, reduced_width, model_per_device)
    cached_state = fetched[2].reshape(
        per_device_share, groups_dev, per_group, head_size, state_size
    )
    cached_x = fetched[3].reshape(per_device_share, tap_count - 1, hidden_features_on_card)
    cached_bc = fetched[4].reshape(per_device_share, tap_count - 1, groups_dev, 2, state_size)
    conv_x = causal_conv(
        cached_x,
        inner_input.reshape(per_device_share, length_value, hidden_features_on_card),
        inner_conv_taps,
    )
    conv_bc = causal_conv(
        cached_bc,
        projection_input.reshape(per_device_share, length_value, groups_dev, 2, state_size),
        projection_conv_taps,
    )
    b_proj = conv_bc[:, :, :, 0]
    c_proj = conv_bc[:, :, :, 1]
    step_size = jax.nn.softplus(step_before_bias.astype(jnp.float32) + step_bias).reshape(
        per_device_share, length_value, heads_dev
    )
    log_decay = jnp.cumsum(-head_decay_rate * step_size, axis=1)
    log_decay5 = log_decay.reshape(per_device_share, length_value, groups_dev, per_group)
    step_size5 = step_size.reshape(per_device_share, length_value, groups_dev, per_group)
    score_bc = jnp.einsum("rtgn,rsgn->rgts", c_proj, b_proj, preferred_element_type=jnp.float32)
    decay_rows = jnp.transpose(log_decay5, (0, 2, 3, 1))
    log_gap = decay_rows[..., :, None] - decay_rows[..., None, :]
    token_ids = jnp.arange(length_value, dtype=jnp.int32)
    causal = token_ids[:, None] >= token_ids[None, :]
    decay_factor = jnp.exp(jnp.where(causal, log_gap, -jnp.inf))
    step_rows = jnp.transpose(step_size5, (0, 2, 3, 1))
    mix_weights = (score_bc[:, :, None] * decay_factor * step_rows[..., None, :]).astype(
        jnp.bfloat16
    )
    conv_heads = conv_x.reshape(per_device_share, length_value, groups_dev, per_group, head_size)
    intra = jnp.einsum(
        "rghts,rsghp->rtghp", mix_weights, conv_heads, preferred_element_type=jnp.float32
    )
    inter = (
        jnp.einsum("rtgn,rghpn->rtghp", c_proj, cached_state, preferred_element_type=jnp.float32)
        * jnp.exp(log_decay5)[..., None]
    )
    skip_gain = head_skip_gain.reshape(groups_dev, per_group)[..., None]
    mixed = intra + inter + skip_gain * conv_heads
    mean_square = jnp.mean(mixed * mixed, axis=(3, 4), keepdims=True)
    normed_output = (
        (mixed * lax.rsqrt(mean_square + NORM_EPSILON)).reshape(
            per_device_share, length_value, hidden_features_on_card
        )
        * group_norm_gain
    ).astype(jnp.bfloat16)
    low_partial = jnp.einsum(
        "rtc,rcq->rtq", normed_output, down_panel, preferred_element_type=jnp.float32
    )
    reduced_rank = lax.psum(low_partial, "head").astype(jnp.bfloat16)
    adapter_output_term = (
        jnp.einsum("rtq,rqd->rtd", reduced_rank, up_panel, preferred_element_type=jnp.float32)
        * ADAPTER_SCALE
    ).astype(jnp.bfloat16)
    log_total = log_decay[:, -1:, :]
    carry_weight = (jnp.exp(log_total - log_decay) * step_size).reshape(
        per_device_share, length_value, groups_dev, per_group
    )
    carried = (conv_heads * carry_weight[..., None]).astype(jnp.bfloat16)
    fresh_state = jnp.einsum(
        "rsghp,rsgn->rghpn", carried, b_proj, preferred_element_type=jnp.float32
    )
    keep_factor = jnp.exp(log_total[:, 0]).reshape(per_device_share, groups_dev, per_group)[
        ..., None, None
    ]
    updated_state = fresh_state + keep_factor * cached_state
    return (
        normed_output.reshape(per_device_share * length_value, hidden_features_on_card),
        adapter_output_term.reshape(per_device_share * length_value, model_per_device),
        updated_state.reshape(per_device_share, heads_dev, head_size, state_size).astype(
            jnp.bfloat16
        ),
    )


def solution(mesh):
    return jax.shard_map(
        per_device,
        mesh=mesh,
        in_specs=(
            P("req", "head"),
            P("req", "head", None, None),
            P("req", "head"),
            P(None, "head"),
            P(None, "head", None, None),
            P("head"),
            P("head"),
            P("head"),
            P("head"),
            P("req"),
            P(),
            P("req"),
            P("req"),
            P("req", "head", None),
            P("req", None, "head"),
            P("req", "head", None, None),
            P("req", None, "head"),
            P("req", None, "head", None, None),
        ),
        out_specs=(P("req", "head"), P("req", "head"), P("req", "head", None, None)),
        check_vma=False,
    )
```

profile of v0, /device:TPU:13, one launch (start us, length us, event | category | flops | bytes accessed | tf_op | source)
XLA Modules:
  0.0 375.6 jit_solution(10896021765367634918)
XLA Ops:
  2.1 6.6 %all-to-all-start.2 = ((bf16[2,16,192]{2,0,1:T(2,128)(2,1)}), bf16[2,16,192]{2,0,1:T(2,128)(2,1)S(1)}, u32[]{:S(2)}, u32[]{:S(2)}) async-start(bf16[2,16,192]{2,0,1:T(2,128)(2,1)} %copy.117), calls=%async_computation.2 | async-start | bytes 32768 | tf_op jit(solution)/shard_map/all_to_all | solution.py:84
  14.2 8.8 %all-reduce.3 = (s32[16]{0:T(128)S(1)}, s32[16]{0:T(128)S(1)}, s32[16]{0:T(128)S(1)}) all-reduce(s32[16]{0:T(128)S(1)} %dynamic-update-slice.1, s32[16]{0:T(128)S(1)} %dynamic-update-slice, s32[16]{0:T(128)S(1)} %dynamic-update-slice.2), channel_id=1, replica_groups=mesh['req'=16,'head'=2] {'req'}, use_global_device_ids=true, to_apply=%add.1 | all-reduce | flops 48 | bytes 384
  23.0 5.5 %all-to-all-start = ((bf16[2,16,1536]{2,0,1:T(2,128)(2,1)}), bf16[2,16,1536]{2,0,1:T(2,128)(2,1)S(1)}, u32[]{:S(2)}, u32[]{:S(2)}) async-start(bf16[2,16,1536]{2,0,1:T(2,128)(2,1)} %bitcast.162), calls=%async_computation | async-start | bytes 196608 | tf_op jit(solution)/shard_map/all_to_all | solution.py:83
  33.3 5.1 %all-to-all-start.3 = ((bf16[16,1,192]{2,1,0:T(2,128)(2,1)}), bf16[16,1,192]{2,1,0:T(2,128)(2,1)S(1)}, u32[]{:S(2)}, u32[]{:S(2)}) async-start(bf16[16,1,192]{2,1,0:T(2,128)(2,1)} %copy.118), calls=%async_computation.3 | async-start | bytes 32768 | tf_op jit(solution)/shard_map/all_to_all | solution.py:96
  43.4 5.4 %all-to-all-start.1 = ((bf16[16,2,768]{2,1,0:T(2,128)(2,1)}), bf16[16,2,768]{2,1,0:T(2,128)(2,1)S(1)}, u32[]{:S(2)}, u32[]{:S(2)}) async-start(bf16[16,2,768]{2,1,0:T(2,128)(2,1)} %reshape.575), calls=%async_computation.1 | async-start | bytes 98304 | tf_op jit(solution)/shard_map/all_to_all | solution.py:95
  56.2 6.9 %all-to-all-start.8 = ((bf16[16,2,8192]{2,1,0:T(2,128)(2,1)}), bf16[16,2,8192]{2,1,0:T(2,128)(2,1)}, u32[]{:S(2)}, u32[]{:S(2)}) async-start(bf16[16,2,8192]{2,1,0:T(2,128)(2,1)} %reshape.579), calls=%async_computation.8 | async-start | bytes 1048576 | tf_op jit(solution)/shard_map/all_to_all | solution.py:75
  64.9 4.8 %all_to_all.129 = bf16[1,16,32768]{2,0,1:T(2,128)(2,1)S(1)} reshape(bf16[1,8192,64]{2,1,0:T(8,128)(2,1)} %copy.133) | data formatting | bytes 2097152 | tf_op jit(solution)/shard_map/all_to_all | solution.py:68
  69.7 7.0 %reduce.14 = bf16[16,32768]{1,0:T(8,128)(2,1)S(1)} reduce(bf16[16,1,32768]{2,1,0:T(2,128)(2,1)S(1)} %bitcast.146, bf16[]{:T(256)} %broadcast.309), dimensions={1}, to_apply=%bitcast.123.reduce_sub_computation | reduce | bytes 2097154
  78.4 7.0 %all-to-all-start.6 = ((bf16[16,2,16384]{2,1,0:T(2,128)(2,1)}), bf16[16,2,16384]{2,1,0:T(2,128)(2,1)S(1)}, u32[]{:S(2)}, u32[]{:S(2)}) async-start(bf16[16,2,16384]{2,1,0:T(2,128)(2,1)} %reshape.583), calls=%async_computation.6 | async-start | bytes 2097152 | tf_op jit(solution)/shard_map/all_to_all | solution.py:68
  86.2 5.5 %all_to_all.116 = bf16[2,16,65536]{2,1,0:T(8,128)(2,1)} reshape(bf16[2,128,64,128]{3,2,1,0:T(8,128)(2,1)} %param.33) | data formatting | bytes 8388608 | tf_op jit(solution)/shard_map/all_to_all | solution.py:82
  91.8 8.5 %copy.129 = bf16[2,16,65536]{2,0,1:T(2,128)(2,1)} copy(bf16[2,16,65536]{2,1,0:T(8,128)(2,1)} %all_to_all.116) | data formatting | bytes 8388608 | tf_op jit(solution)/shard_map/all_to_all | solution.py:82
  100.4 7.5 %all-to-all-done.6 = bf16[16,2,16384]{2,1,0:T(2,128)(2,1)S(1)} async-done(((bf16[16,2,16384]{2,1,0:T(2,128)(2,1)}), bf16[16,2,16384]{2,1,0:T(2,128)(2,1)S(1)}, u32[]{:S(2)}, u32[]{:S(2)}) %all-to-all-start.6) | async-done | bytes 1048608 | tf_op jit(solution)/shard_map/all_to_all | solution.py:68
  107.9 4.7 %all-to-all-start.4 = ((bf16[2,16,65536]{2,0,1:T(2,128)(2,1)}), bf16[2,16,65536]{2,0,1:T(2,128)(2,1)}, u32[]{:S(2)}, u32[]{:S(2)}) async-start(bf16[2,16,65536]{2,0,1:T(2,128)(2,1)} %copy.129), calls=%async_computation.4 | async-start | bytes 8388608 | tf_op jit(solution)/shard_map/all_to_all | solution.py:82
  116.1 6.4 %copy.113 = bf16[256,8192]{0,1:T(8,128)(2,1)} copy(bf16[256,8192]{1,0:T(8,128)(2,1)} %param.18) | data formatting | bytes 8388608 | tf_op args[0]
  139.4 5.8 %reshape.584 = bf16[16,1,32768]{2,1,0:T(2,128)(2,1)} reshape(bf16[16,2,16384]{2,1,0:T(2,128)(2,1)} %copy-done.3) | data formatting | bytes 2097152
  150.2 55.5 %all-to-all-done.4 = bf16[2,16,65536]{2,0,1:T(2,128)(2,1)} async-done(((bf16[2,16,65536]{2,0,1:T(2,128)(2,1)}), bf16[2,16,65536]{2,0,1:T(2,128)(2,1)}, u32[]{:S(2)}, u32[]{:S(2)}) %all-to-all-start.4) | async-done | bytes 4194336 | tf_op jit(solution)/shard_map/all_to_all | solution.py:82
  205.7 4.3 %all-to-all-start.9 = ((bf16[16,2,8192]{2,1,0:T(2,128)(2,1)}), bf16[16,2,8192]{2,1,0:T(2,128)(2,1)}, u32[]{:S(2)}, u32[]{:S(2)}) async-start(bf16[16,2,8192]{2,1,0:T(2,128)(2,1)} %reshape.581), calls=%async_computation.9 | async-start | bytes 1048576 | tf_op jit(solution)/shard_map/all_to_all | solution.py:93
  216.2 5.4 %all_to_all.119 = bf16[32,65536]{1,0:T(8,128)(2,1)} reshape(bf16[16,2,65536]{2,1,0:T(2,128)(2,1)} %bitcast.39) | data formatting | bytes 8388608 | tf_op jit(solution)/shard_map/all_to_all | solution.py:82
  221.6 7.8 %gather_fusion.2 = bf16[16,65536]{1,0:T(8,128)(2,1)} fusion(bf16[32,65536]{1,0:T(8,128)(2,1)} %all_to_all.119, s32[1024]{0:T(1024)} %copy-done.25), kind=kCustom, calls=%fused_computation.2 | custom fusion | bytes 4194368 | tf_op jit(solution)/shard_map/jit(_take)/gather | solution.py:88
  229.4 6.3 %all-to-all-start.7 = ((bf16[16,2,16384]{2,1,0:T(2,128)(2,1)}), bf16[16,2,16384]{2,1,0:T(2,128)(2,1)S(1)}, u32[]{:S(2)}, u32[]{:S(2)}) async-start(bf16[16,2,16384]{2,1,0:T(2,128)(2,1)} %reshape.585), calls=%async_computation.7 | async-start | bytes 2097152 | tf_op jit(solution)/shard_map/all_to_all | solution.py:92
  238.9 4.5 %reduce.11 = bf16[16,65536]{1,0:T(8,128)(2,1)} reduce(bf16[16,1,65536]{2,0,1:T(8,128)(2,1)} %bitcast_select_fusion, bf16[]{:T(256)} %broadcast.309), dimensions={1}, to_apply=%copy.130.reduce_sub_computation | reduce | bytes 4194306 | tf_op jit(solution)/shard_map/jit(_take)/select_n | solution.py:88
  247.4 13.1 %all-to-all-done.7 = bf16[16,2,16384]{2,1,0:T(2,128)(2,1)S(1)} async-done(((bf16[16,2,16384]{2,1,0:T(2,128)(2,1)}), bf16[16,2,16384]{2,1,0:T(2,128)(2,1)S(1)}, u32[]{:S(2)}, u32[]{:S(2)}) %all-to-all-start.7) | async-done | bytes 1048608 | tf_op jit(solution)/shard_map/all_to_all | solution.py:92
  260.5 4.6 %all-to-all-start.5 = ((bf16[16,2,32768]{2,1,0:T(2,128)(2,1)}), bf16[16,2,32768]{2,1,0:T(2,128)(2,1)}, u32[]{:S(2)}, u32[]{:S(2)}) async-start(bf16[16,2,32768]{2,1,0:T(2,128)(2,1)} %reshape.577), calls=%async_computation.5 | async-start | bytes 4194304 | tf_op jit(solution)/shard_map/all_to_all | solution.py:94
  265.1 14.2 %multiply_convert_fusion.5 = bf16[1,256,8192]{1,2,0:T(8,128)(2,1)S(1)} fusion(bf16[256,8192]{0,1:T(8,128)(2,1)} %copy.113, bf16[1,256,8192]{1,2,0:T(8,128)(2,1)} %bitcast.139, bf16[1,3,8192]{1,2,0:T(8,128)(2,1)S(1)} %copy.114, f32[8192]{0:T(1024)S(1)} %bitcast.157, f32[8192]{0:T(1024)S(1)} %bitcast.158, f32[8192]{0:T(1024)S(1)} %bitcast.156, ...), kind=kLoop, calls=%fused_computation.22 | loop fusion | flops 52428800 | bytes 12763136 | tf_op jit(solution)/shard_map/convert_element_type | solution.py:16
  281.3 10.8 %fusion = f32[4,32,64,256]{3,2,1,0:T(8,128)} fusion(bf16[256,4,32,64]{0,3,2,1:T(8,128)(2,1)S(1)} %bitcast.141, f32[4,32,256]{2,1,0:T(8,128)S(1)} %bitcast.161, f32[4,32,256]{2,1,0:T(8,128)S(1)} %bitcast.160, f32[4,256,256]{2,1,0:T(8,128)S(1)} %copy-done.11, pred[256,256]{1,0:T(8,128)(4,1)S(1)} %copy-done.18), kind=kOutput, calls=%fused_computation.6 | convolution fusion | flops 1115684864 | bytes 13959168 | tf_op jit(solution)/shard_map/rghts,rsghp->rtghp/dot_general | solution.py:134
  300.3 6.4 %reduce.4 = bf16[16,32768]{1,0:T(8,128)(2,1)S(1)} reduce(bf16[16,1,32768]{2,1,0:T(2,128)(2,1)S(1)} %reshape.586, bf16[]{:T(256)} %constant.116), dimensions={1}, to_apply=%all_to_all.124.reduce_sub_computation | reduce | bytes 2097154 | tf_op jit(solution)/shard_map/all_to_all | solution.py:92
  313.1 10.4 %reshape.578 = bf16[16,1,65536]{2,1,0:T(2,128)(2,1)} reshape(bf16[16,2,32768]{2,1,0:T(2,128)(2,1)} %all-to-all-done.5) | data formatting | bytes 4194304
  323.6 13.7 %reduce.3 = bf16[16,65536]{1,0:T(8,128)(2,1)} reduce(bf16[16,1,65536]{2,1,0:T(2,128)(2,1)} %reshape.578, bf16[]{:T(256)} %constant.116), dimensions={1}, to_apply=%all_to_all.120.reduce_sub_computation | reduce | bytes 4194306 | tf_op jit(solution)/shard_map/all_to_all | solution.py:94
  339.5 5.8 %multiply_reduce_fusion = (f32[256,4]{0,1:T(4,128)S(1)}, f32[1,256,4,32,64]{1,4,3,2,0:T(8,128)S(1)}) fusion(bf16[1,256,4,32,64]{1,4,3,2,0:T(8,128)(2,1)} %bitcast.142, f32[4,32]{1,0:T(4,128)S(1)} %copy-done.21, f32[256,4,32]{0,2,1:T(8,128)S(1)} %bitcast.152, bf16[4,32,64,128]{3,2,1,0:T(8,128)(2,1)S(1)} %reshape.496, ...), kind=kOutput, calls=%fused_computation.21 | convolution fusion | flops 551549952 | bytes 23468032 | tf_op jit(solution)/shard_map/rtgn,rghpn->rtghp/dot_general | solution.py:138
  350.5 4.9 %psum.7 = bf16[1,256,64]{1,2,0:T(8,128)(2,1)S(1)} all-reduce(f32[1,256,64]{1,2,0:T(8,128)S(1)} %convolution_bitcast_fusion), channel_id=1, replica_groups=mesh['req'=16,'head'=2] {'head'}, use_global_device_ids=true, to_apply=%region_4.5 | all-reduce | flops 16384 | bytes 98304 | tf_op jit(solution)/shard_map/psum | solution.py:153
  355.4 8.9 %copy.132 = f32[256,8192]{1,0:T(8,128)} copy(f32[256,8192]{0,1:T(8,128)} %bitcast.140) | data formatting | bytes 16777216 | tf_op jit(solution)/shard_map/reshape | solution.py:145
  364.3 6.3 %multiply_convert_fusion.4 = bf16[256,8192]{1,0:T(8,128)(2,1)} fusion(f32[256,8192]{1,0:T(8,128)} %copy.132, f32[8192]{0:T(1024)S(1)} %copy-done.13), kind=kLoop, calls=%fused_computation.20 | loop fusion | flops 4194304 | bytes 12615680 | tf_op jit(solution)/shard_map/convert_element_type | solution.py:149
  (159 shorter events, 93.8 us)
Async XLA Ops:
  0.6 62.5 %copy-start.10 = (bf16[1,8192,64]{1,2,0:T(8,128)(2,1)S(1)}, bf16[1,8192,64]{1,2,0:T(8,128)(2,1)}, u32[]{:S(2)}) copy-start(bf16[1,8192,64]{1,2,0:T(8,128)(2,1)} %param.31) | copy-start | bytes 3145732
  2.1 20.9 %all-to-all-start.2 = ((bf16[2,16,192]{2,0,1:T(2,128)(2,1)}), bf16[2,16,192]{2,0,1:T(2,128)(2,1)S(1)}, u32[]{:S(2)}, u32[]{:S(2)}) async-start(bf16[2,16,192]{2,0,1:T(2,128)(2,1)} %copy.117), calls=%async_computation.2 | async-start | bytes 32768 | tf_op jit(solution)/shard_map/all_to_all | solution.py:84
  23.0 19.8 %copy-start.23 = (pred[16]{0:T(512)(128)(4,1)}, pred[16]{0:T(512)(128)(4,1)S(1)}, u32[]{:S(2)}) copy-start(pred[16]{0:T(512)(128)(4,1)S(1)} %get-tuple-element.10) | copy-start | bytes 52
  23.0 19.8 %copy-start.25 = (s32[1024]{0:T(1024)}, s32[1024]{0:T(1024)S(1)}, u32[]{:S(2)}) copy-start(s32[1024]{0:T(1024)S(1)} %pad_clamp_fusion.1) | copy-start | bytes 12292
  23.0 10.3 %all-to-all-start = ((bf16[2,16,1536]{2,0,1:T(2,128)(2,1)}), bf16[2,16,1536]{2,0,1:T(2,128)(2,1)S(1)}, u32[]{:S(2)}, u32[]{:S(2)}) async-start(bf16[2,16,1536]{2,0,1:T(2,128)(2,1)} %bitcast.162), calls=%async_computation | async-start | bytes 196608 | tf_op jit(solution)/shard_map/all_to_all | solution.py:83
  33.3 9.4 %all-to-all-start.3 = ((bf16[16,1,192]{2,1,0:T(2,128)(2,1)}), bf16[16,1,192]{2,1,0:T(2,128)(2,1)S(1)}, u32[]{:S(2)}, u32[]{:S(2)}) async-start(bf16[16,1,192]{2,1,0:T(2,128)(2,1)} %copy.118), calls=%async_computation.3 | async-start | bytes 32768 | tf_op jit(solution)/shard_map/all_to_all | solution.py:96
  43.4 12.8 %all-to-all-start.1 = ((bf16[16,2,768]{2,1,0:T(2,128)(2,1)}), bf16[16,2,768]{2,1,0:T(2,128)(2,1)S(1)}, u32[]{:S(2)}, u32[]{:S(2)}) async-start(bf16[16,2,768]{2,1,0:T(2,128)(2,1)} %reshape.575), calls=%async_computation.1 | async-start | bytes 98304 | tf_op jit(solution)/shard_map/all_to_all | solution.py:95
  56.2 22.2 %all-to-all-start.8 = ((bf16[16,2,8192]{2,1,0:T(2,128)(2,1)}), bf16[16,2,8192]{2,1,0:T(2,128)(2,1)}, u32[]{:S(2)}, u32[]{:S(2)}) async-start(bf16[16,2,8192]{2,1,0:T(2,128)(2,1)} %reshape.579), calls=%async_computation.8 | async-start | bytes 1048576 | tf_op jit(solution)/shard_map/all_to_all | solution.py:75
  69.7 15.7 %copy-start.30 = (f32[128]{0:T(128)S(1)}, f32[128]{0:T(128)}, u32[]{:S(2)}) copy-start(f32[128]{0:T(128)} %param.24) | copy-start | bytes 1540
  69.7 15.7 %copy-start.29 = (f32[128]{0:T(128)S(1)}, f32[128]{0:T(128)}, u32[]{:S(2)}) copy-start(f32[128]{0:T(128)} %param.25) | copy-start | bytes 1540
  69.7 16.4 %copy-start.22 = (f32[4,4,2,128]{3,2,1,0:T(2,128)S(1)}, f32[4,4,2,128]{3,2,1,0:T(2,128)}, u32[]{:S(2)}) copy-start(f32[4,4,2,128]{3,2,1,0:T(2,128)} %param.22) | copy-start | bytes 49156
  69.7 16.4 %copy-start.13 = (f32[8192]{0:T(1024)S(1)}, f32[8192]{0:T(1024)}, u32[]{:S(2)}) copy-start(f32[8192]{0:T(1024)} %param.26) | copy-start | bytes 98308
  78.4 29.5 %all-to-all-start.6 = ((bf16[16,2,16384]{2,1,0:T(2,128)(2,1)}), bf16[16,2,16384]{2,1,0:T(2,128)(2,1)S(1)}, u32[]{:S(2)}, u32[]{:S(2)}) async-start(bf16[16,2,16384]{2,1,0:T(2,128)(2,1)} %reshape.583), calls=%async_computation.6 | async-start | bytes 2097152 | tf_op jit(solution)/shard_map/all_to_all | solution.py:68
  91.7 8.5 %copy-start.12 = (bf16[256,128]{1,0:T(8,128)(2,1)S(1)}, bf16[256,128]{1,0:T(8,128)(2,1)}, u32[]{:S(2)}) copy-start(bf16[256,128]{1,0:T(8,128)(2,1)} %param.20) | copy-start | bytes 196612
  91.7 8.5 %copy-start.26 = (f32[128]{0:T(128)S(1)}, f32[128]{0:T(128)}, u32[]{:S(2)}) copy-start(f32[128]{0:T(128)} %param.23) | copy-start | bytes 1540
  100.4 15.6 %copy-start.8 = (bf16[256,4,2,128]{3,2,1,0:T(2,128)(2,1)S(1)}, bf16[256,4,2,128]{3,2,1,0:T(2,128)(2,1)}, u32[]{:S(2)}) copy-start(bf16[256,4,2,128]{3,2,1,0:T(2,128)(2,1)} %param.19) | copy-start | bytes 1572868
  107.9 97.8 %all-to-all-start.4 = ((bf16[2,16,65536]{2,0,1:T(2,128)(2,1)}), bf16[2,16,65536]{2,0,1:T(2,128)(2,1)}, u32[]{:S(2)}, u32[]{:S(2)}) async-start(bf16[2,16,65536]{2,0,1:T(2,128)(2,1)} %copy.129), calls=%async_computation.4 | async-start | bytes 8388608 | tf_op jit(solution)/shard_map/all_to_all | solution.py:82
  116.1 6.5 %copy-start.31 = (s32[16]{0:T(128)S(1)}, s32[16]{0:T(128)}, u32[]{:S(2)}) copy-start(s32[16]{0:T(128)} %param.28) | copy-start | bytes 196
  116.1 8.4 %copy-start.14 = (f32[4,8192]{1,0:T(4,128)S(1)}, f32[4,8192]{1,0:T(4,128)}, u32[]{:S(2)}) copy-start(f32[4,8192]{1,0:T(4,128)} %param.21) | copy-start | bytes 393220
  116.1 8.5 %copy-start.20 = (bf16[16,1,192]{2,1,0:T(2,128)(2,1)S(1)}, bf16[16,1,192]{2,1,0:T(2,128)(2,1)}, u32[]{:S(2)}) copy-start(bf16[16,1,192]{2,1,0:T(2,128)(2,1)} %copy-done.19) | copy-start | bytes 18436
  205.7 23.7 %all-to-all-start.9 = ((bf16[16,2,8192]{2,1,0:T(2,128)(2,1)}), bf16[16,2,8192]{2,1,0:T(2,128)(2,1)}, u32[]{:S(2)}, u32[]{:S(2)}) async-start(bf16[16,2,8192]{2,1,0:T(2,128)(2,1)} %reshape.581), calls=%async_computation.9 | async-start | bytes 1048576 | tf_op jit(solution)/shard_map/all_to_all | solution.py:93
  221.6 14.1 %copy-start.24 = (pred[16]{0:T(512)(128)(4,1)S(1)}, pred[16]{0:T(512)(128)(4,1)}, u32[]{:S(2)}) copy-start(pred[16]{0:T(512)(128)(4,1)} %copy-done.23) | copy-start | bytes 52
  229.4 31.1 %all-to-all-start.7 = ((bf16[16,2,16384]{2,1,0:T(2,128)(2,1)}), bf16[16,2,16384]{2,1,0:T(2,128)(2,1)S(1)}, u32[]{:S(2)}, u32[]{:S(2)}) async-start(bf16[16,2,16384]{2,1,0:T(2,128)(2,1)} %reshape.585), calls=%async_computation.7 | async-start | bytes 2097152 | tf_op jit(solution)/shard_map/all_to_all | solution.py:92
  260.5 18.8 %copy-start.4 = (bf16[16,2,16384]{2,1,0:T(2,128)(2,1)}, bf16[16,2,16384]{2,1,0:T(2,128)(2,1)S(1)}, u32[]{:S(2)}) copy-start(bf16[16,2,16384]{2,1,0:T(2,128)(2,1)S(1)} %all-to-all-done.7) | copy-start | bytes 3145732
  260.5 52.6 %all-to-all-start.5 = ((bf16[16,2,32768]{2,1,0:T(2,128)(2,1)}), bf16[16,2,32768]{2,1,0:T(2,128)(2,1)}, u32[]{:S(2)}, u32[]{:S(2)}) async-start(bf16[16,2,32768]{2,1,0:T(2,128)(2,1)} %reshape.577), calls=%async_computation.5 | async-start | bytes 4194304 | tf_op jit(solution)/shard_map/all_to_all | solution.py:94
  265.1 16.2 %copy-start.11 = (f32[4,256,256]{2,1,0:T(8,128)S(1)}, f32[4,256,256]{2,1,0:T(8,128)}, u32[]{:S(2)}) copy-start(f32[4,256,256]{2,1,0:T(8,128)} %fusion.18) | copy-start | bytes 3145732
  265.1 16.2 %copy-start.16 = (f32[1,256,128]{1,2,0:T(8,128)S(1)}, f32[1,256,128]{1,2,0:T(8,128)}, u32[]{:S(2)}) copy-start(f32[1,256,128]{1,2,0:T(8,128)} %copy.127) | copy-start | bytes 393220
  265.1 16.2 %copy-start.17 = (f32[256,128]{0,1:T(8,128)S(1)}, f32[256,128]{0,1:T(8,128)}, u32[]{:S(2)}) copy-start(f32[256,128]{0,1:T(8,128)} %copy.128) | copy-start | bytes 393220
  265.1 16.2 %copy-start.18 = (pred[256,256]{1,0:T(8,128)(4,1)S(1)}, pred[256,256]{1,0:T(8,128)(4,1)}, u32[]{:S(2)}) copy-start(pred[256,256]{1,0:T(8,128)(4,1)} %iota_compare_fusion) | copy-start | bytes 196612
  292.1 6.7 %copy-start.5 = (bf16[16,2,16384]{2,1,0:T(2,128)(2,1)S(1)}, bf16[16,2,16384]{2,1,0:T(2,128)(2,1)}, u32[]{:S(2)}) copy-start(bf16[16,2,16384]{2,1,0:T(2,128)(2,1)} %copy-done.4) | copy-start | bytes 3145732
  323.6 15.9 %copy-start.7 = (bf16[1,256,4,2,128]{4,1,2,3,0:T(8,128)(2,1)S(1)}, bf16[1,256,4,2,128]{4,1,2,3,0:T(8,128)(2,1)}, u32[]{:S(2)}) copy-start(bf16[1,256,4,2,128]{4,1,2,3,0:T(8,128)(2,1)} %copy-done.6) | copy-start | bytes 1572868
  323.6 15.9 %copy-start.21 = (f32[4,32]{1,0:T(4,128)S(1)}, f32[4,32]{1,0:T(4,128)}, u32[]{:S(2)}) copy-start(f32[4,32]{1,0:T(4,128)} %mul.259) | copy-start | bytes 1540
  (10 other events, 40.2 us)
where the time goes:
time: 383 us; the launch traced here: 376 us
  local copies, waits for them, and re-layouts  117 us (31%)
  waiting for transfers between devices  84.5 us (22%)
  other arithmetic  76.9 us (20%)
  starting transfers between devices  56.5 us (15%)
  matrix products  23.6 us (6%)
  blocking collectives  13.7 us (4%)
    all_to_all x1, waiting for transfers between devices, per_device(): lax.all_to_all(ssm_flat, 'req', split_axis=1, concat_axis=0, tiled=True)  55.5 us
    unnamed x88, local copies, waits for them, and re-layouts  54.5 us
    all_to_all x3, local copies, waits for them, and re-layouts, per_device(): lax.all_to_all(ssm_flat, 'req', split_axis=1, concat_axis=0, tiled=True)  19.5 us
    convert_element_type x2, other arithmetic, causal_conv(): return jax.nn.silu(summed).astype(jnp.bfloat16)  14.9 us
    all_to_all x1, other arithmetic, per_device(): lax.all_to_all(chosen_state, 'req', split_axis=0, concat_axis=1, tiled=True)  13.7 us
    all_to_all x1, waiting for transfers between devices, per_device(): lax.all_to_all(picked_left_factor, 'req', split_axis=0, concat_axis=1, ti...  13.1 us
    unnamed x2, other arithmetic  10.8 us
    dot_general x1, matrix products, per_device(): jnp.einsum('rghts,rsghp->rtghp', mix_weights, conv_heads, preferred_eleme...  10.8 us
  transfers between devices with their start and end apart: 10, of which 6 were waited for; matrix products, arithmetic and copies ran while one was open for 36% of the time, Pallas kernels for 0%

commit v1 on v0

--- a/solution.py
+++ b/solution.py
@@ -48,60 +48,61 @@
     model_per_device = adapter_up_panels.shape[2]
     tap_count = inner_conv_taps.shape[0]
     length_value = inner_input.shape[0] // per_device_share
-    tenant_all, owner_all, slot_all = (
-        lax.all_gather(tenant, "req", axis=0, tiled=True),
-        lax.all_gather(cache_holder_index, "req", axis=0, tiled=True),
-        lax.all_gather(cache_slot_index, "req", axis=0, tiled=True),
-    )
-    customer_identifiers = jnp.arange(tenant_adapter_row.shape[0], dtype=jnp.int32)
-    picked_customer_matrix_pair = jnp.sum(
-        jnp.where(
-            tenant_all[:, None] == customer_identifiers[None, :], tenant_adapter_row[None, :], 0
-        ),
+    n = lax.axis_size("req")
+    me = lax.axis_index("req")
+    rows = slots_dev * (tap_count - 1)
+    numbers = jnp.stack([tenant, cache_holder_index, cache_slot_index], axis=1)
+    numbers = numbers.reshape(1, -1).astype(jnp.bfloat16)
+    numbers = jnp.pad(numbers, ((0, rows - 1), (0, 128 - numbers.shape[1])))
+    small = jnp.concatenate(
+        [
+            inner_conv_cache.reshape(rows, hidden_features_on_card),
+            projection_conv_cache.reshape(rows, groups_dev * 2 * state_size),
+            numbers,
+        ],
         axis=1,
     )
-    ssm_flat = cached_ssm_states.reshape(slots_dev, -1)
-    convx_flat = inner_conv_cache.reshape(slots_dev, -1)
-    convbc_flat = projection_conv_cache.reshape(slots_dev, -1)
-    cache_pick = owner_all * slots_dev + slot_all
-    dispersion_factor = (
-        lax.all_to_all(
-            adapter_down_panels.reshape(adapter_down_panels.shape[0], -1),
-            "req",
-            split_axis=1,
-            concat_axis=0,
-            tiled=True,
-        ),
-        lax.all_to_all(
-            adapter_up_panels.reshape(adapter_up_panels.shape[0], -1),
-            "req",
-            split_axis=1,
-            concat_axis=0,
-            tiled=True,
-        ),
-        lax.all_to_all(ssm_flat, "req", split_axis=1, concat_axis=0, tiled=True),
-        lax.all_to_all(convx_flat, "req", split_axis=1, concat_axis=0, tiled=True),
-        lax.all_to_all(convbc_flat, "req", split_axis=1, concat_axis=0, tiled=True),
-    )
-    picked_left_factor = jnp.take(dispersion_factor[0], picked_customer_matrix_pair, axis=0)
-    picked_right_factor = jnp.take(dispersion_factor[1], picked_customer_matrix_pair, axis=0)
-    chosen_state = jnp.take(dispersion_factor[2], cache_pick, axis=0)
-    chosen_convx = jnp.take(dispersion_factor[3], cache_pick, axis=0)
-    chosen_convbc = jnp.take(dispersion_factor[4], cache_pick, axis=0)
-    fetched = (
-        lax.all_to_all(picked_left_factor, "req", split_axis=0, concat_axis=1, tiled=True),
-        lax.all_to_all(picked_right_factor, "req", split_axis=0, concat_axis=1, tiled=True),
-        lax.all_to_all(chosen_state, "req", split_axis=0, concat_axis=1, tiled=True),
-        lax.all_to_all(chosen_convx, "req", split_axis=0, concat_axis=1, tiled=True),
-        lax.all_to_all(chosen_convbc, "req", split_axis=0, concat_axis=1, tiled=True),
-    )
-    down_panel = fetched[0].reshape(per_device_share, hidden_features_on_card, reduced_width)
-    up_panel = fetched[1].reshape(per_device_share, reduced_width, model_per_device)
-    cached_state = fetched[2].reshape(
+    panels = jnp.concatenate(
+        [
+            jnp.transpose(adapter_down_panels[0].reshape(n, -1, reduced_width), (0, 2, 1)),
+            jnp.transpose(adapter_up_panels[0].reshape(reduced_width, n, -1), (1, 0, 2)),
+        ],
+        axis=2,
+    )
+    down_piece = hidden_features_on_card // n
+    panels = lax.all_to_all(panels, "req", split_axis=0, concat_axis=0, tiled=True)
+    small_all = lax.all_gather(small, "req", axis=0, tiled=False)
+    index_base = small.shape[1] - 128
+    meta = small_all[:, 0, index_base : index_base + 3].astype(jnp.int32)
+    tenant_all, owner_all, slot_all = meta[:, 0], meta[:, 1], meta[:, 2]
+    picked_row = jnp.take(tenant_adapter_row, tenant_all, axis=0, mode="clip")
+    my_slot = jnp.sum(jnp.where(owner_all == me, slot_all, 0))
+    my_state = lax.dynamic_index_in_dim(cached_ssm_states, my_slot, 0, keepdims=False)
+    state_pieces = my_state.reshape(n, heads_dev * head_size // n, state_size)
+    state_pieces = lax.all_to_all(state_pieces, "req", split_axis=0, concat_axis=0, tiled=True)
+    state_pieces = jnp.take(state_pieces, owner_all, axis=0, mode="clip")
+    state_pieces = lax.all_to_all(state_pieces, "req", split_axis=0, concat_axis=0, tiled=True)
+    panels = jnp.take(panels, picked_row, axis=0, mode="clip")
+    panels, state_pieces = lax.optimization_barrier((panels, state_pieces))
+    panels = lax.all_to_all(panels, "req", split_axis=0, concat_axis=0, tiled=True)
+    down_t = jnp.transpose(panels[:, :, :down_piece], (1, 0, 2)).reshape(
+        reduced_width, hidden_features_on_card
+    )
+    up_panel = jnp.transpose(panels[:, :, down_piece:], (1, 0, 2)).reshape(
+        per_device_share, reduced_width, model_per_device
+    )
+    cached_state = state_pieces.reshape(
         per_device_share, groups_dev, per_group, head_size, state_size
     )
-    cached_x = fetched[3].reshape(per_device_share, tap_count - 1, hidden_features_on_card)
-    cached_bc = fetched[4].reshape(per_device_share, tap_count - 1, groups_dev, 2, state_size)
+    mine = lax.dynamic_slice(
+        small_all,
+        (cache_holder_index[0], cache_slot_index[0] * (tap_count - 1), 0),
+        (1, tap_count - 1, small.shape[1]),
+    )
+    cached_x = mine[:, :, :hidden_features_on_card]
+    cached_bc = mine[:, :, hidden_features_on_card:index_base].reshape(
+        1, tap_count - 1, groups_dev, 2, state_size
+    )
     conv_x = causal_conv(
         cached_x,
         inner_input.reshape(per_device_share, length_value, hidden_features_on_card),
@@ -148,7 +149,7 @@
         * group_norm_gain
     ).astype(jnp.bfloat16)
     low_partial = jnp.einsum(
-        "rtc,rcq->rtq", normed_output, down_panel, preferred_element_type=jnp.float32
+        "rtc,qc->rtq", normed_output, down_t, preferred_element_type=jnp.float32
     )
     reduced_rank = lax.psum(low_partial, "head").astype(jnp.bfloat16)
     adapter_output_term = (

time: 383 us -> 262 us (0.68); the launches traced: 376 us -> 261 us
  local copies, waits for them, and re-layouts: 117 us -> 44.1 us
  other arithmetic: 76.9 us -> 29.1 us
  starting transfers between devices: 56.5 us -> 20 us
  waiting for transfers between devices: 84.5 us -> 118 us
  between operations: 3.34 us -> 18.3 us
  blocking collectives: 13.7 us -> 4.92 us
    all_gather x0 -> x1, waiting for transfers between devices: none -> 62.3 us  [per_device(): small_all = lax.all_gather(small, 'req', axis=0, tiled=False)]
    all_to_all x10 -> x4, starting transfers between devices: 56.5 us -> 20 us  [the longest x2 11.1 us: per_device(): lax.all_to_all(panels, 'req', split_axis=0, concat_axis=0, tiled=True)]
    unnamed x88 -> x49, local copies, waits for them, and re-layouts: 54.5 us -> 18.9 us
    all_to_all x10 -> x4, waiting for transfers between devices: 84.5 us -> 56 us  [the longest x2 47 us: per_device(): lax.all_to_all(state_pieces, 'req', split_axis=0, concat_axis=0, tiled=True)]
    all_to_all x9 -> x0, local copies, waits for them, and re-layouts: 28.3 us -> none  [the longest x3 19.5 us: per_device(): lax.all_to_all(ssm_flat, 'req', split_axis=1, concat_axis=0, tiled=True)]
    all_to_all x5 -> x0, other arithmetic: 23.5 us -> none  [the longest x1 13.7 us: per_device(): lax.all_to_all(chosen_state, 'req', split_axis=0, concat_axis=1, tiled=True)]
    select_n x10 -> x0, other arithmetic: 14.9 us -> none  [the longest x2 7.67 us: per_device(): chosen_state = jnp.take(dispersion_factor[2], cache_pick, axis=0)]
    unnamed x2 -> x1, other arithmetic: 10.8 us -> 0.69 us
  transfers between devices with their start and end apart: 10 -> 5, of which waited for: 6 -> 4; matrix products, arithmetic and copies ran while one was open for 36% -> 33% of each run, Pallas kernels for 0% -> 0%
where the time goes in v1:
time: 262 us; the launch traced here: 261 us
  waiting for transfers between devices  118 us (45%)
  local copies, waits for them, and re-layouts  44.1 us (17%)
  other arithmetic  29.1 us (11%)
  matrix products  25.9 us (10%)
  starting transfers between devices  20 us (8%)
  between operations  18.3 us (7%)
  blocking collectives  4.92 us (2%)
    all_gather x1, waiting for transfers between devices, per_device(): small_all = lax.all_gather(small, 'req', axis=0, tiled=False)  62.3 us
    all_to_all x2, waiting for transfers between devices, per_device(): lax.all_to_all(state_pieces, 'req', split_axis=0, concat_axis=0, tiled=True)  47 us
    unnamed x49, local copies, waits for them, and re-layouts  18.9 us
    convert_element_type x2, other arithmetic, causal_conv(): return jax.nn.silu(summed).astype(jnp.bfloat16)  17.3 us
    all_to_all x2, starting transfers between devices, per_device(): lax.all_to_all(panels, 'req', split_axis=0, concat_axis=0, tiled=True)  11.1 us
    dot_general x1, matrix products, per_device(): jnp.einsum('rghts,rsghp->rtghp', mix_weights, conv_heads, preferred_eleme...  10.9 us
    all_to_all x2, waiting for transfers between devices, per_device(): lax.all_to_all(panels, 'req', split_axis=0, concat_axis=0, tiled=True)  9.02 us
    reshape x1, local copies, waits for them, and re-layouts, per_device(): (mixed * lax.rsqrt(mean_square + NORM_EPSILON)).reshape(per_device_share,...  8.91 us
  transfers between devices with their start and end apart: 5, of which 4 were waited for; matrix products, arithmetic and copies ran while one was open for 33% of the time, Pallas kernels for 0%

profile of v1, /device:TPU:13, one launch (start us, length us, event | category | flops | bytes accessed | tf_op | source)
XLA Modules:
  0.0 260.7 jit_solution(9919035498303486846)
XLA Ops:
  9.9 1.0 copy.104
  11.8 1.1 copy.140
  13.1 1.6 copy.139
  15.3 1.3 pad_maximum_fusion.1
  16.6 6.6 %all-to-all-start = ((bf16[16,64,768]{2,1,0:T(8,128)(2,1)}), bf16[16,64,768]{2,1,0:T(8,128)(2,1)S(1)}, u32[]{:S(2)}, u32[]{:S(2)}) async-start(bf16[16,64,768]{2,1,0:T(8,128)(2,1)} %pad_maximum_fusion.1), calls=%async_computation | async-start | bytes 3145728 | tf_op jit(solution)/shard_map/all_to_all | solution.py:73
  24.8 62.3 %all-gather.4.cloned.1.call-done = bf16[16,6,9344]{2,1,0:T(8,128)(2,1)} async-done(((bf16[1,6,9344]{2,1,0:T(8,128)(2,1)}), bf16[16,6,9344]{2,1,0:T(8,128)(2,1)}) %all-gather.4.cloned.1.call-update) | async-done | bytes 1794064 | tf_op jit(solution)/shard_map/all_gather | solution.py:74
  90.6 3.1 %constant_dynamic-slice_fusion.1 = bf16[1,128,64,128]{3,2,1,0:T(8,128)(2,1)} fusion(bf16[2,128,64,128]{3,2,1,0:T(8,128)(2,1)} %param.33, s32[]{:T(128)S(6)} %select_n.31), kind=kLoop, calls=%fused_computation.94 | loop fusion | bytes 4194308 | tf_op jit(solution)/shard_map/jit(dynamic_index_in_dim)/dynamic_slice | solution.py:80
  93.7 1.1 copy-done.5
  94.9 4.6 %all-to-all-start.1 = ((bf16[16,512,128]{2,1,0:T(8,128)(2,1)}), bf16[16,512,128]{2,1,0:T(8,128)(2,1)S(1)}, u32[]{:S(2)}, u32[]{:S(2)}) async-start(bf16[16,512,128]{2,1,0:T(8,128)(2,1)} %bitcast.43), calls=%async_computation.1 | async-start | bytes 4194304 | tf_op jit(solution)/shard_map/all_to_all | solution.py:82
  101.9 6.4 %copy.106 = bf16[256,8192]{0,1:T(8,128)(2,1)} copy(bf16[256,8192]{1,0:T(8,128)(2,1)} %param.18) | data formatting | bytes 8388608 | tf_op args[0]
  111.2 1.8 copy.134
  113.7 3.3 %gather_fusion.1 = bf16[16,64,768]{2,1,0:T(8,128)(2,1)} fusion(bf16[16,64,768]{2,1,0:T(8,128)(2,1)} %copy-done.5, s32[1024]{0:T(1024)S(1)} %pad_clamp_fusion.1), kind=kCustom, calls=%fused_computation.1 | custom fusion | bytes 3145792 | tf_op jit(solution)/shard_map/jit(_take)/gather | solution.py:85
  117.0 2.5 multiply_convert_fusion.9
  119.5 1.3 fusion.18
  120.8 26.6 %all-to-all-done.1 = bf16[16,512,128]{2,1,0:T(8,128)(2,1)S(1)} async-done(((bf16[16,512,128]{2,1,0:T(8,128)(2,1)}), bf16[16,512,128]{2,1,0:T(8,128)(2,1)S(1)}, u32[]{:S(2)}, u32[]{:S(2)}) %all-to-all-start.1) | async-done | bytes 2097184 | tf_op jit(solution)/shard_map/all_to_all | solution.py:82
  147.4 2.1 gather_fusion.2
  149.5 4.3 %all-to-all-start.2 = ((bf16[16,512,128]{2,1,0:T(8,128)(2,1)}), bf16[16,512,128]{2,1,0:T(8,128)(2,1)S(1)}, u32[]{:S(2)}, u32[]{:S(2)}) async-start(bf16[16,512,128]{2,1,0:T(8,128)(2,1)} %gather_fusion.2), calls=%async_computation.2 | async-start | bytes 4194304 | tf_op jit(solution)/shard_map/all_to_all | solution.py:84
  153.8 14.8 %multiply_convert_fusion.5 = bf16[1,256,8192]{1,2,0:T(8,128)(2,1)S(1)} fusion(bf16[256,8192]{0,1:T(8,128)(2,1)} %copy.106, bf16[1,256,8192]{1,2,0:T(8,128)(2,1)} %bitcast.148, bf16[1,3,8192]{1,2,0:T(8,128)(2,1)} %copy.134, f32[8192]{0:T(1024)S(1)} %bitcast.172, f32[8192]{0:T(1024)S(1)} %bitcast.173, f32[8192]{0:T(1024)S(1)} %bitcast.171, f32[8192]{0:T(1024)S(1)} %bitcast.170), kind=kLoop, calls=%fused_computation.20 | loop fusion | flops 52428800 | bytes 12763136 | tf_op jit(solution)/shard_map/convert_element_type | solution.py:16
  168.7 2.0 copy-done.3
  170.7 10.9 %fusion = f32[4,32,64,256]{3,2,1,0:T(8,128)} fusion(bf16[256,4,32,64]{0,3,2,1:T(8,128)(2,1)S(1)} %bitcast.150, f32[4,32,256]{2,1,0:T(8,128)S(1)} %bitcast.176, f32[4,32,256]{2,1,0:T(8,128)S(1)} %bitcast.174, f32[4,256,256]{2,1,0:T(8,128)S(1)} %copy-done.7, pred[256,256]{1,0:T(8,128)(4,1)S(1)} %copy-done.14), kind=kOutput, calls=%fused_computation.4 | convolution fusion | flops 1115684864 | bytes 13959168 | tf_op jit(solution)/shard_map/rghts,rsghp->rtghp/dot_general | solution.py:135
  181.6 20.4 %all-to-all-done.2 = bf16[16,512,128]{2,1,0:T(8,128)(2,1)S(1)} async-done(((bf16[16,512,128]{2,1,0:T(8,128)(2,1)}), bf16[16,512,128]{2,1,0:T(8,128)(2,1)S(1)}, u32[]{:S(2)}, u32[]{:S(2)}) %all-to-all-start.2) | async-done | bytes 2097184 | tf_op jit(solution)/shard_map/all_to_all | solution.py:84
  201.9 4.5 %all-to-all-start.3 = ((bf16[16,64,768]{2,1,0:T(8,128)(2,1)}), bf16[16,64,768]{2,1,0:T(8,128)(2,1)}, u32[]{:S(2)}, u32[]{:S(2)}) async-start(bf16[16,64,768]{2,1,0:T(8,128)(2,1)} %gather_fusion.1), calls=%async_computation.3 | async-start | bytes 3145728 | tf_op jit(solution)/shard_map/all_to_all | solution.py:87
  206.4 5.8 %multiply_reduce_fusion = (f32[256,4]{0,1:T(4,128)S(1)}, f32[1,256,4,32,64]{1,4,3,2,0:T(8,128)S(1)}) fusion(bf16[1,256,4,32,64]{1,4,3,2,0:T(8,128)(2,1)} %bitcast.151, f32[4,32]{1,0:T(4,128)S(1)} %mul.263, f32[256,4,32]{0,2,1:T(8,128)S(1)} %bitcast.167, bf16[4,32,64,128]{3,2,1,0:T(8,128)(2,1)S(1)} %bitcast.154, ...), kind=kOutput, calls=%fused_computation.19 | convolution fusion | flops 551549952 | bytes 23468032 | tf_op jit(solution)/shard_map/rtgn,rghpn->rtghp/dot_general | solution.py:139
  212.3 5.3 %multiply_convert_fusion.3 = (bf16[1,256,4,32,64]{1,4,3,2,0:T(8,128)(2,1)}, f32[1,256,4,32,64]{1,4,3,2,0:T(8,128)}) fusion(f32[4,32,64]{2,1,0:T(8,128)S(1)} %mul.271, f32[1,256,4,32,64]{1,4,3,2,0:T(8,128)S(1)} %get-tuple-element.27, f32[256,4]{0,1:T(4,128)S(1)} %add_rsqrt_fusion), kind=kLoop, calls=%fused_computation.17 | loop fusion | flops 6291456 | bytes 21008384 | tf_op jit(solution)/shard_map/convert_element_type | solution.py:150
  217.6 8.9 %copy.124 = f32[256,8192]{1,0:T(8,128)} copy(f32[256,8192]{0,1:T(8,128)} %bitcast.149) | data formatting | bytes 16777216 | tf_op jit(solution)/shard_map/reshape | solution.py:146
  226.5 5.1 %add_convert_fusion = bf16[4,32,64,128]{3,2,1,0:T(8,128)(2,1)} fusion(bf16[4,32,64,128]{3,2,1,0:T(8,128)(2,1)S(1)} %bitcast.155, f32[4,32]{1,0:T(4,128)S(1)} %exp.53, bf16[256,4,32,64]{0,3,2,1:T(8,128)(2,1)} %bitcast.152, f32[256,4,32]{0,2,1:T(8,128)S(1)} %bitcast.175, bf16[1,256,4,2,128]{4,1,2,3,0:T(8,128)(2,1)S(1)} %multiply_convert_fusion.9), kind=kOutput, calls=%fused_computation.31 | convolution fusion | flops 547356672 | bytes 8783872 | tf_op jit(solution)/shard_map/rsghp,rsgn->rghpn/dot_general | solution.py:164
  231.6 2.8 %multiply_convert_fusion.4 = bf16[256,8192]{1,0:T(8,128)(2,1)} fusion(f32[256,8192]{1,0:T(8,128)S(1)} %copy-done.2, f32[8192]{0:T(1024)S(1)} %copy-done.9), kind=kLoop, calls=%fused_computation.18 | loop fusion | flops 4194304 | bytes 12615680 | tf_op jit(solution)/shard_map/convert_element_type | solution.py:150
  234.4 9.0 %all-to-all-done.3 = bf16[16,64,768]{2,1,0:T(8,128)(2,1)} async-done(((bf16[16,64,768]{2,1,0:T(8,128)(2,1)}), bf16[16,64,768]{2,1,0:T(8,128)(2,1)}, u32[]{:S(2)}, u32[]{:S(2)}) %all-to-all-start.3) | async-done | bytes 1572896 | tf_op jit(solution)/shard_map/all_to_all | solution.py:87
  243.4 1.5 slice_bitcast_fusion
  244.9 1.1 slice_bitcast_fusion.1
  246.9 4.9 %psum.7 = bf16[1,256,64]{1,2,0:T(8,128)(2,1)S(1)} all-reduce(f32[1,256,64]{1,2,0:T(8,128)S(1)} %convolution_bitcast_fusion), channel_id=1, replica_groups=mesh['req'=16,'head'=2] {'head'}, use_global_device_ids=true, to_apply=%region_4.5 | all-reduce | flops 16384 | bytes 98304 | tf_op jit(solution)/shard_map/psum | solution.py:154
  251.8 2.0 fusion.9
  (87 shorter events, 12.4 us)
Async XLA Ops:
  7.2 105.9 %copy-start = (s32[16]{0:T(128)S(1)}, s32[16]{0:T(128)}, u32[]{:S(2)}) copy-start(s32[16]{0:T(128)} %param.28) | copy-start | bytes 196
  7.2 79.9 %all-gather.4.cloned.1.call-start = ((), (), s32[]{:S(2)}) async-start(), calls=%async_computation.4 | async-start | bytes 2541568 | tf_op jit(solution)/shard_map/all_gather | solution.py:74
  14.7 8.5 %copy-start.18 = (f32[128]{0:T(128)S(1)}, f32[128]{0:T(128)}, u32[]{:S(2)}) copy-start(f32[128]{0:T(128)} %param.24) | copy-start | bytes 1540
  14.7 8.5 %copy-start.17 = (f32[128]{0:T(128)S(1)}, f32[128]{0:T(128)}, u32[]{:S(2)}) copy-start(f32[128]{0:T(128)} %param.25) | copy-start | bytes 1540
  14.7 8.6 %copy-start.15 = (f32[4,4,2,128]{3,2,1,0:T(2,128)S(1)}, f32[4,4,2,128]{3,2,1,0:T(2,128)}, u32[]{:S(2)}) copy-start(f32[4,4,2,128]{3,2,1,0:T(2,128)} %param.22) | copy-start | bytes 49156
  14.7 8.7 %copy-start.9 = (f32[8192]{0:T(1024)S(1)}, f32[8192]{0:T(1024)}, u32[]{:S(2)}) copy-start(f32[8192]{0:T(1024)} %param.26) | copy-start | bytes 98308
  14.7 8.7 %copy-start.8 = (bf16[256,128]{1,0:T(8,128)(2,1)S(1)}, bf16[256,128]{1,0:T(8,128)(2,1)}, u32[]{:S(2)}) copy-start(bf16[256,128]{1,0:T(8,128)(2,1)} %param.20) | copy-start | bytes 196612
  14.7 8.7 %copy-start.16 = (f32[128]{0:T(128)S(1)}, f32[128]{0:T(128)}, u32[]{:S(2)}) copy-start(f32[128]{0:T(128)} %param.23) | copy-start | bytes 1540
  16.6 77.1 %all-to-all-start = ((bf16[16,64,768]{2,1,0:T(8,128)(2,1)}), bf16[16,64,768]{2,1,0:T(8,128)(2,1)S(1)}, u32[]{:S(2)}, u32[]{:S(2)}) async-start(bf16[16,64,768]{2,1,0:T(8,128)(2,1)} %pad_maximum_fusion.1), calls=%async_computation | async-start | bytes 3145728 | tf_op jit(solution)/shard_map/all_to_all | solution.py:73
  90.6 10.5 %copy-start.6 = (bf16[256,4,2,128]{3,2,1,0:T(2,128)(2,1)S(1)}, bf16[256,4,2,128]{3,2,1,0:T(2,128)(2,1)}, u32[]{:S(2)}) copy-start(bf16[256,4,2,128]{3,2,1,0:T(2,128)(2,1)} %param.19) | copy-start | bytes 1572868
  93.7 1.1 copy-start.5
  94.9 52.5 %all-to-all-start.1 = ((bf16[16,512,128]{2,1,0:T(8,128)(2,1)}), bf16[16,512,128]{2,1,0:T(8,128)(2,1)S(1)}, u32[]{:S(2)}, u32[]{:S(2)}) async-start(bf16[16,512,128]{2,1,0:T(8,128)(2,1)} %bitcast.43), calls=%async_computation.1 | async-start | bytes 4194304 | tf_op jit(solution)/shard_map/all_to_all | solution.py:82
  101.9 7.1 %copy-start.10 = (f32[4,8192]{1,0:T(4,128)S(1)}, f32[4,8192]{1,0:T(4,128)}, u32[]{:S(2)}) copy-start(f32[4,8192]{1,0:T(4,128)} %param.21) | copy-start | bytes 393220
  149.5 52.4 %all-to-all-start.2 = ((bf16[16,512,128]{2,1,0:T(8,128)(2,1)}), bf16[16,512,128]{2,1,0:T(8,128)(2,1)S(1)}, u32[]{:S(2)}, u32[]{:S(2)}) async-start(bf16[16,512,128]{2,1,0:T(8,128)(2,1)} %gather_fusion.2), calls=%async_computation.2 | async-start | bytes 4194304 | tf_op jit(solution)/shard_map/all_to_all | solution.py:84
  153.8 16.9 %copy-start.7 = (f32[4,256,256]{2,1,0:T(8,128)S(1)}, f32[4,256,256]{2,1,0:T(8,128)}, u32[]{:S(2)}) copy-start(f32[4,256,256]{2,1,0:T(8,128)} %fusion.18) | copy-start | bytes 3145732
  153.8 16.9 %copy-start.11 = (f32[1,256,128]{1,2,0:T(8,128)S(1)}, f32[1,256,128]{1,2,0:T(8,128)}, u32[]{:S(2)}) copy-start(f32[1,256,128]{1,2,0:T(8,128)} %copy.118) | copy-start | bytes 393220
  153.8 16.9 %copy-start.13 = (f32[256,128]{0,1:T(8,128)S(1)}, f32[256,128]{0,1:T(8,128)}, u32[]{:S(2)}) copy-start(f32[256,128]{0,1:T(8,128)} %copy.119) | copy-start | bytes 393220
  153.8 16.9 %copy-start.14 = (pred[256,256]{1,0:T(8,128)(4,1)S(1)}, pred[256,256]{1,0:T(8,128)(4,1)}, u32[]{:S(2)}) copy-start(pred[256,256]{1,0:T(8,128)(4,1)} %iota_compare_fusion) | copy-start | bytes 196612
  168.6 2.0 copy-start.3
  201.9 41.4 %all-to-all-start.3 = ((bf16[16,64,768]{2,1,0:T(8,128)(2,1)}), bf16[16,64,768]{2,1,0:T(8,128)(2,1)}, u32[]{:S(2)}, u32[]{:S(2)}) async-start(bf16[16,64,768]{2,1,0:T(8,128)(2,1)} %gather_fusion.1), calls=%async_computation.3 | async-start | bytes 3145728 | tf_op jit(solution)/shard_map/all_to_all | solution.py:87
  217.6 8.9 %copy-start.12 = (f32[1,256,128]{1,2,0:T(8,128)S(1)}, f32[1,256,128]{1,2,0:T(8,128)}, u32[]{:S(2)}) copy-start(f32[1,256,128]{1,2,0:T(8,128)} %copy.127) | copy-start | bytes 393220
  226.5 5.1 %copy-start.2 = (f32[256,8192]{1,0:T(8,128)S(1)}, f32[256,8192]{1,0:T(8,128)}, u32[]{:S(2)}) copy-start(f32[256,8192]{1,0:T(8,128)} %copy.124) | copy-start | bytes 25165828
  243.4 2.7 %copy-start.4 = (bf16[1,256,4,32,64]{1,4,3,2,0:T(8,128)(2,1)S(1)}, bf16[1,256,4,32,64]{1,4,3,2,0:T(8,128)(2,1)}, u32[]{:S(2)}) copy-start(bf16[1,256,4,32,64]{1,4,3,2,0:T(8,128)(2,1)} %get-tuple-element.7) | copy-start | bytes 12582916
  246.0 7.8 %copy-start.1 = (s32[16]{0:T(128)S(1)}, s32[16]{0:T(128)}, u32[]{:S(2)}) copy-start(s32[16]{0:T(128)} %param.28) | copy-start | bytes 196
Sparse Core Ops, SparseCore 0:
  11.9 75.1 all-gather.3

commit v2 on v1

--- a/solution.py
+++ b/solution.py
@@ -1,6 +1,10 @@
+import functools
+
 import jax
 import jax.numpy as jnp
 from jax import lax
+from jax.experimental import pallas as pl
+from jax.experimental.pallas import tpu as pltpu
 from jax.sharding import PartitionSpec as P
 
 ADAPTER_SCALE = 2.0
@@ -14,6 +18,130 @@
     for tap in range(1, weight.shape[0]):
         summed = summed + weight[tap] * joined[:, tap : tap + length_value]
     return jax.nn.silu(summed).astype(jnp.bfloat16)
+
+
+def exchange_kernel(
+    n,
+    numbers_ref,
+    small_ref,
+    meta_ref,
+    conv_ref,
+    meta_land,
+    landed,
+    picked,
+    conv_land,
+    table,
+    meta_send,
+    meta_recv,
+    first_send,
+    first_recv,
+    second_send,
+    second_recv,
+    table_sem,
+):
+    me = lax.axis_index("req")
+
+    def peer_of(step):
+        return lax.rem(me + step, n)
+
+    def remote(src, dst, send, recv, step):
+        return pltpu.make_async_remote_copy(
+            src_ref=src,
+            dst_ref=dst,
+            send_sem=send.at[step],
+            recv_sem=recv.at[step],
+            device_id={"req": peer_of(step)},
+            device_id_type=pl.DeviceIdType.MESH,
+        )
+
+    def meta_copy(step):
+        return remote(numbers_ref, meta_land.at[me], meta_send, meta_recv, step)
+
+    def first_copy(step):
+        return remote(small_ref.at[peer_of(step)], landed.at[me], first_send, first_recv, step)
+
+    def second_copy(step):
+        return remote(picked.at[peer_of(step)], conv_land.at[me], second_send, second_recv, step)
+
+    barrier = pltpu.get_barrier_semaphore()
+
+    def greet(step, carry):
+        pl.semaphore_signal(
+            barrier,
+            inc=1,
+            device_id={"req": peer_of(step)},
+            device_id_type=pl.DeviceIdType.MESH,
+        )
+        return carry
+
+    lax.fori_loop(1, n, greet, 0)
+    pl.semaphore_wait(barrier, n - 1)
+
+    def send_first(step, carry):
+        meta_copy(step).start()
+        first_copy(step).start()
+        return carry
+
+    lax.fori_loop(1, n, send_first, 0)
+    meta_land[me] = numbers_ref[...]
+    landed[me] = small_ref[me]
+
+    def wait_first(step, carry):
+        meta_copy(step).wait()
+        first_copy(step).wait()
+        return carry
+
+    lax.fori_loop(1, n, wait_first, 0)
+    to_table = pltpu.make_async_copy(meta_land, table, table_sem)
+    to_table.start()
+    to_table.wait()
+
+    def pick(request):
+        return landed[table[request, 0, 1], table[request, 0, 2]]
+
+    def send_second(step, carry):
+        peer = peer_of(step)
+        picked[peer] = pick(peer)
+        second_copy(step).start()
+        return carry
+
+    lax.fori_loop(1, n, send_second, 0)
+    conv_land[me] = pick(me)
+
+    def wait_second(step, carry):
+        second_copy(step).wait()
+        return carry
+
+    lax.fori_loop(1, n, wait_second, 0)
+    meta_ref[...] = meta_land[...]
+    conv_ref[...] = conv_land[...]
+
+
+def exchange(n, numbers, small):
+    slots, rows = small.shape[1], small.shape[2]
+    in_vmem = pl.BlockSpec(memory_space=pltpu.VMEM)
+    return pl.pallas_call(
+        functools.partial(exchange_kernel, n),
+        out_shape=(
+            jax.ShapeDtypeStruct((n, 8, 128), jnp.int32),
+            jax.ShapeDtypeStruct((n, rows, 128), jnp.bfloat16),
+        ),
+        in_specs=[in_vmem, in_vmem],
+        out_specs=(in_vmem, in_vmem),
+        scratch_shapes=[
+            pltpu.VMEM((n, 8, 128), jnp.int32),
+            pltpu.VMEM((n, slots, rows, 128), jnp.bfloat16),
+            pltpu.VMEM((n, rows, 128), jnp.bfloat16),
+            pltpu.VMEM((n, rows, 128), jnp.bfloat16),
+            pltpu.SMEM((n, 8, 128), jnp.int32),
+        ]
+        + [pltpu.SemaphoreType.DMA((n,))] * 6
+        + [pltpu.SemaphoreType.DMA],
+        compiler_params=pltpu.CompilerParams(collective_id=0, has_side_effects=True),
+        cost_estimate=pl.CostEstimate(
+            flops=0, bytes_accessed=30_000_000, transcendentals=0
+        ),
+    )(numbers, small)
 
 
 def per_device(
@@ -50,18 +178,17 @@
     length_value = inner_input.shape[0] // per_device_share
     n = lax.axis_size("req")
     me = lax.axis_index("req")
-    rows = slots_dev * (tap_count - 1)
-    numbers = jnp.stack([tenant, cache_holder_index, cache_slot_index], axis=1)
-    numbers = numbers.reshape(1, -1).astype(jnp.bfloat16)
-    numbers = jnp.pad(numbers, ((0, rows - 1), (0, 128 - numbers.shape[1])))
-    small = jnp.concatenate(
-        [
-            inner_conv_cache.reshape(rows, hidden_features_on_card),
-            projection_conv_cache.reshape(rows, groups_dev * 2 * state_size),
-            numbers,
-        ],
+    x_size = (tap_count - 1) * hidden_features_on_card
+    flat = jnp.concatenate(
+        [inner_conv_cache.reshape(slots_dev, -1), projection_conv_cache.reshape(slots_dev, -1)],
         axis=1,
     )
+    flat_size = flat.shape[1]
+    tiles = -(-flat_size // (n * 2048))
+    small = jnp.pad(flat, ((0, 0), (0, n * tiles * 2048 - flat_size)))
+    small = jnp.transpose(small.reshape(slots_dev, n, tiles * 16, 128), (1, 0, 2, 3))
+    numbers = jnp.concatenate([tenant, cache_holder_index, cache_slot_index])
+    numbers = jnp.broadcast_to(jnp.pad(numbers, (0, 128 - numbers.shape[0])), (8, 128))
     panels = jnp.concatenate(
         [
             jnp.transpose(adapter_down_panels[0].reshape(n, -1, reduced_width), (0, 2, 1)),
@@ -71,10 +198,8 @@
     )
     down_piece = hidden_features_on_card // n
     panels = lax.all_to_all(panels, "req", split_axis=0, concat_axis=0, tiled=True)
-    small_all = lax.all_gather(small, "req", axis=0, tiled=False)
-    index_base = small.shape[1] - 128
-    meta = small_all[:, 0, index_base : index_base + 3].astype(jnp.int32)
-    tenant_all, owner_all, slot_all = meta[:, 0], meta[:, 1], meta[:, 2]
+    meta, conv_pieces = exchange(n, numbers, small)
+    tenant_all, owner_all, slot_all = meta[:, 0, 0], meta[:, 0, 1], meta[:, 0, 2]
     picked_row = jnp.take(tenant_adapter_row, tenant_all, axis=0, mode="clip")
     my_slot = jnp.sum(jnp.where(owner_all == me, slot_all, 0))
     my_state = lax.dynamic_index_in_dim(cached_ssm_states, my_slot, 0, keepdims=False)
@@ -94,15 +219,9 @@
     cached_state = state_pieces.reshape(
         per_device_share, groups_dev, per_group, head_size, state_size
     )
-    mine = lax.dynamic_slice(
-        small_all,
-        (cache_holder_index[0], cache_slot_index[0] * (tap_count - 1), 0),
-        (1, tap_count - 1, small.shape[1]),
-    )
-    cached_x = mine[:, :, :hidden_features_on_card]
-    cached_bc = mine[:, :, hidden_features_on_card:index_base].reshape(
-        1, tap_count - 1, groups_dev, 2, state_size
-    )
+    mine = conv_pieces.reshape(1, -1)
+    cached_x = mine[:, :x_size].reshape(1, tap_count - 1, hidden_features_on_card)
+    cached_bc = mine[:, x_size:flat_size].reshape(1, tap_count - 1, groups_dev, 2, state_size)
     conv_x = causal_conv(
         cached_x,
         inner_input.reshape(per_device_share, length_value, hidden_features_on_card),

time: 262 us -> 230 us (0.88)
  waiting for transfers between devices: 118 us -> 83 us
  Pallas kernels: 0 us -> 16.6 us
  between operations: 18.3 us -> 5.03 us
    all_gather x1 -> x0, waiting for transfers between devices: 62.3 us -> none  [per_device(): small_all = lax.all_gather(small, 'req', axis=0, tiled=False)]
    all_to_all x2, waiting for transfers between devices: 9.02 us -> 26.6 us  [per_device(): lax.all_to_all(panels, 'req', split_axis=0, concat_axis=0, tiled=True)]
    pallas_call x0 -> x1, Pallas kernels: none -> 16.6 us  [exchange(): pl.pallas_call(functools.partial(exchange_kernel, n), out_shape=(jax.Shap...]
    all_to_all x2, waiting for transfers between devices: 47 us -> 56.4 us  [per_device(): lax.all_to_all(state_pieces, 'req', split_axis=0, concat_axis=0, tiled=True)]
    unnamed x49 -> x69, local copies, waits for them, and re-layouts: 18.9 us -> 14.3 us
  transfers between devices with their start and end apart: 5 -> 4, of which waited for: 4 -> 4; matrix products, arithmetic and copies ran while one was open for 33% -> 37% of each run, Pallas kernels for 0% -> 0%
where the time goes in v2:
time: 230 us; the launch traced here: 229 us
  waiting for transfers between devices  83 us (36%)
  local copies, waits for them, and re-layouts  44.7 us (19%)
  other arithmetic  30.5 us (13%)
  matrix products  26 us (11%)
  starting transfers between devices  18.3 us (8%)
  Pallas kernels  16.6 us (7%)
  between operations  5.03 us (2%)
  blocking collectives  4.92 us (2%)
    all_to_all x2, waiting for transfers between devices, per_device(): lax.all_to_all(state_pieces, 'req', split_axis=0, concat_axis=0, tiled=True)  56.4 us
    all_to_all x2, waiting for transfers between devices, per_device(): lax.all_to_all(panels, 'req', split_axis=0, concat_axis=0, tiled=True)  26.6 us
    convert_element_type x2, other arithmetic, causal_conv(): return jax.nn.silu(summed).astype(jnp.bfloat16)  17.2 us
    pallas_call x1, Pallas kernels, exchange(): pl.pallas_call(functools.partial(exchange_kernel, n), out_shape=(jax.Shap...  16.6 us
    unnamed x69, local copies, waits for them, and re-layouts  14.3 us
    dot_general x1, matrix products, per_device(): jnp.einsum('rghts,rsghp->rtghp', mix_weights, conv_heads, preferred_eleme...  10.9 us
    all_to_all x2, starting transfers between devices, per_device(): lax.all_to_all(state_pieces, 'req', split_axis=0, concat_axis=0, tiled=True)  9.54 us
    reshape x1, local copies, waits for them, and re-layouts, per_device(): (mixed * lax.rsqrt(mean_square + NORM_EPSILON)).reshape(per_device_share,...  8.96 us
  transfers between devices with their start and end apart: 4, of which 4 were waited for; matrix products, arithmetic and copies ran while one was open for 37% of the time, Pallas kernels for 0%

profile of v2, /device:TPU:13, one launch (start us, length us, event | category | flops | bytes accessed | tf_op | source)
XLA Modules:
  0.0 229.1 jit_solution(12830276589706363699)
XLA Ops:
  5.7 16.6 %shard_map.193 = (s32[16,8,128]{2,1,0:T(8,128)}, bf16[16,16,128]{2,1,0:T(8,128)(2,1)}) custom-call(s32[8,128]{1,0:T(8,128)} %broadcast_in_dim.38.numbers_ref, bf16[16,2,16,128]{3,2,1,0:T(8,128)(2,1)} %bitcast.160), custom_call_target="tpu_custom_call" | custom-call | bytes 30000000 | tf_op jit(solution)/shard_map/pallas_call | solution.py:123
  22.3 2.3 %slice_reduce_fusion.3 = (s32[16]{0:T(128)}, s32[]{:T(128)}, s32[16]{0:T(128)}) fusion(s32[16,8,128]{2,1,0:T(8,128)} %get-tuple-element.8, s32[]{:T(128)S(6)} %axis_index.15), kind=kLoop, calls=%fused_computation.77 | loop fusion | flops 47 | bytes 328 | tf_op jit(solution)/shard_map/slice | solution.py:202
  26.7 3.1 %constant_dynamic-slice_fusion = bf16[1,128,64,128]{3,2,1,0:T(8,128)(2,1)} fusion(bf16[2,128,64,128]{3,2,1,0:T(8,128)(2,1)} %param.33, s32[]{:T(128)S(6)} %select_n.23), kind=kLoop, calls=%fused_computation.91 | loop fusion | bytes 4194308 | tf_op jit(solution)/shard_map/jit(dynamic_index_in_dim)/dynamic_slice | solution.py:205
  29.9 5.9 %all-to-all-start.1 = ((bf16[16,512,128]{2,1,0:T(8,128)(2,1)}), bf16[16,512,128]{2,1,0:T(8,128)(2,1)S(1)}, u32[]{:S(2)}, u32[]{:S(2)}) async-start(bf16[16,512,128]{2,1,0:T(8,128)(2,1)} %bitcast.147), calls=%async_computation.1 | async-start | bytes 4194304 | tf_op jit(solution)/shard_map/all_to_all | solution.py:207
  41.0 1.6 copy.81
  43.2 1.3 pad_maximum_fusion.1
  44.6 39.3 %all-to-all-done.1 = bf16[16,512,128]{2,1,0:T(8,128)(2,1)S(1)} async-done(((bf16[16,512,128]{2,1,0:T(8,128)(2,1)}), bf16[16,512,128]{2,1,0:T(8,128)(2,1)S(1)}, u32[]{:S(2)}, u32[]{:S(2)}) %all-to-all-start.1) | async-done | bytes 2097184 | tf_op jit(solution)/shard_map/all_to_all | solution.py:207
  83.9 4.3 %all-to-all-start = ((bf16[16,64,768]{2,1,0:T(8,128)(2,1)}), bf16[16,64,768]{2,1,0:T(8,128)(2,1)}, u32[]{:S(2)}, u32[]{:S(2)}) async-start(bf16[16,64,768]{2,1,0:T(8,128)(2,1)} %pad_maximum_fusion.1), calls=%async_computation | async-start | bytes 3145728 | tf_op jit(solution)/shard_map/all_to_all | solution.py:200
  88.2 1.2 slice_reduce_fusion
  92.6 1.8 copy.56
  94.5 6.4 %copy.55 = bf16[256,8192]{0,1:T(8,128)(2,1)} copy(bf16[256,8192]{1,0:T(8,128)(2,1)} %param.18) | data formatting | bytes 8388608 | tf_op args[0]
  101.6 2.4 %multiply_convert_fusion.9 = bf16[1,256,4,2,128]{4,1,2,3,0:T(8,128)(2,1)S(1)} fusion(bf16[1,3,4,2,128]{4,1,2,3,0:T(4,128)(2,1)S(1)} %copy.60, bf16[1,256,4,2,128]{4,1,2,3,0:T(8,128)(2,1)} %bitcast.151, f32[4,2,128]{2,0,1:T(4,128)S(1)} %copy-done.21, f32[4,2,128]{2,0,1:T(4,128)S(1)} %copy-done.22, f32[4,2,128]{2,0,1:T(4,128)S(1)} %copy-done.20, ...), kind=kLoop, calls=%fused_computation.39 | loop fusion | flops 6553600 | bytes 1595392 | tf_op jit(solution)/shard_map/convert_element_type | solution.py:20
  104.1 1.3 fusion.20
  105.5 2.1 gather_fusion.2
  107.6 17.7 %all-to-all-done = bf16[16,64,768]{2,1,0:T(8,128)(2,1)} async-done(((bf16[16,64,768]{2,1,0:T(8,128)(2,1)}), bf16[16,64,768]{2,1,0:T(8,128)(2,1)}, u32[]{:S(2)}, u32[]{:S(2)}) %all-to-all-start) | async-done | bytes 1572896 | tf_op jit(solution)/shard_map/all_to_all | solution.py:200
  125.3 3.7 %all-to-all-start.2 = ((bf16[16,512,128]{2,1,0:T(8,128)(2,1)}), bf16[16,512,128]{2,1,0:T(8,128)(2,1)S(1)}, u32[]{:S(2)}, u32[]{:S(2)}) async-start(bf16[16,512,128]{2,1,0:T(8,128)(2,1)} %gather_fusion.2), calls=%async_computation.2 | async-start | bytes 4194304 | tf_op jit(solution)/shard_map/all_to_all | solution.py:209
  129.0 14.8 %multiply_convert_fusion.5 = bf16[1,256,8192]{1,2,0:T(8,128)(2,1)S(1)} fusion(bf16[256,8192]{0,1:T(8,128)(2,1)} %copy.55, bf16[1,256,8192]{1,2,0:T(8,128)(2,1)} %bitcast.139, bf16[1,3,8192]{1,2,0:T(8,128)(2,1)} %copy.56, f32[8192]{0:T(1024)S(1)} %bitcast.165, f32[8192]{0:T(1024)S(1)} %bitcast.166, f32[8192]{0:T(1024)S(1)} %bitcast.164, f32[8192]{0:T(1024)S(1)} %bitcast.163), kind=kLoop, calls=%fused_computation.20 | loop fusion | flops 52428800 | bytes 12763136 | tf_op jit(solution)/shard_map/convert_element_type | solution.py:20
  143.8 2.0 copy-done.3
  145.9 10.9 %fusion = f32[4,32,64,256]{3,2,1,0:T(8,128)} fusion(bf16[256,4,32,64]{0,3,2,1:T(8,128)(2,1)S(1)} %bitcast.141, f32[4,32,256]{2,1,0:T(8,128)S(1)} %bitcast.169, f32[4,32,256]{2,1,0:T(8,128)S(1)} %bitcast.167, f32[4,256,256]{2,1,0:T(8,128)S(1)} %copy-done.6, pred[256,256]{1,0:T(8,128)(4,1)S(1)} %iota_compare_fusion.1), kind=kOutput, calls=%fused_computation.4 | convolution fusion | flops 1115684864 | bytes 13959168 | tf_op jit(solution)/shard_map/rghts,rsghp->rtghp/dot_general | solution.py:254
  156.7 3.2 %gather_fusion.1 = bf16[16,64,768]{2,1,0:T(8,128)(2,1)} fusion(bf16[16,64,768]{2,1,0:T(8,128)(2,1)} %all-to-all-done, s32[1024]{0:T(1024)S(1)} %pad_clamp_fusion.1), kind=kCustom, calls=%fused_computation.1 | custom fusion | bytes 3145792 | tf_op jit(solution)/shard_map/jit(_take)/gather | solution.py:210
  160.0 17.1 %all-to-all-done.2 = bf16[16,512,128]{2,1,0:T(8,128)(2,1)S(1)} async-done(((bf16[16,512,128]{2,1,0:T(8,128)(2,1)}), bf16[16,512,128]{2,1,0:T(8,128)(2,1)S(1)}, u32[]{:S(2)}, u32[]{:S(2)}) %all-to-all-start.2) | async-done | bytes 2097184 | tf_op jit(solution)/shard_map/all_to_all | solution.py:209
  177.1 4.5 %all-to-all-start.3 = ((bf16[16,64,768]{2,1,0:T(8,128)(2,1)}), bf16[16,64,768]{2,1,0:T(8,128)(2,1)}, u32[]{:S(2)}, u32[]{:S(2)}) async-start(bf16[16,64,768]{2,1,0:T(8,128)(2,1)} %gather_fusion.1), calls=%async_computation.3 | async-start | bytes 3145728 | tf_op jit(solution)/shard_map/all_to_all | solution.py:212
  181.6 5.9 %multiply_reduce_fusion = (f32[256,4]{0,1:T(4,128)S(1)}, f32[1,256,4,32,64]{1,4,3,2,0:T(8,128)S(1)}) fusion(bf16[1,256,4,32,64]{1,4,3,2,0:T(8,128)(2,1)} %bitcast.142, f32[4,32]{1,0:T(4,128)S(1)} %mul.255, f32[256,4,32]{0,2,1:T(8,128)S(1)} %bitcast.158, bf16[4,32,64,128]{3,2,1,0:T(8,128)(2,1)S(1)} %bitcast.145, ...), kind=kOutput, calls=%fused_computation.19 | convolution fusion | flops 551549952 | bytes 23468032 | tf_op jit(solution)/shard_map/rtgn,rghpn->rtghp/dot_general | solution.py:258
  187.5 5.3 %multiply_convert_fusion.3 = (bf16[1,256,4,32,64]{1,4,3,2,0:T(8,128)(2,1)}, f32[1,256,4,32,64]{1,4,3,2,0:T(8,128)}) fusion(f32[4,32,64]{2,1,0:T(8,128)S(1)} %copy-done.9, f32[1,256,4,32,64]{1,4,3,2,0:T(8,128)S(1)} %get-tuple-element.31, f32[256,4]{0,1:T(4,128)S(1)} %add_rsqrt_fusion), kind=kLoop, calls=%fused_computation.17 | loop fusion | flops 6291456 | bytes 21008384 | tf_op jit(solution)/shard_map/convert_element_type | solution.py:269
  192.8 9.0 %copy.72 = f32[256,8192]{1,0:T(8,128)} copy(f32[256,8192]{0,1:T(8,128)} %bitcast.140) | data formatting | bytes 16777216 | tf_op jit(solution)/shard_map/reshape | solution.py:265
  201.8 5.1 %add_convert_fusion = bf16[4,32,64,128]{3,2,1,0:T(8,128)(2,1)} fusion(bf16[4,32,64,128]{3,2,1,0:T(8,128)(2,1)S(1)} %bitcast.146, f32[4,32]{1,0:T(4,128)S(1)} %copy-done.26, bf16[256,4,32,64]{0,3,2,1:T(8,128)(2,1)} %bitcast.143, f32[256,4,32]{0,2,1:T(8,128)S(1)} %bitcast.168, bf16[1,256,4,2,128]{4,1,2,3,0:T(8,128)(2,1)S(1)} %multiply_convert_fusion.9), kind=kOutput, calls=%fused_computation.31 | convolution fusion | flops 547356672 | bytes 8783872 | tf_op jit(solution)/shard_map/rsghp,rsgn->rghpn/dot_general | solution.py:283
  206.9 2.7 %multiply_convert_fusion.4 = bf16[256,8192]{1,0:T(8,128)(2,1)} fusion(f32[256,8192]{1,0:T(8,128)S(1)} %copy-done.2, f32[8192]{0:T(1024)S(1)} %copy-done.13), kind=kLoop, calls=%fused_computation.18 | loop fusion | flops 4194304 | bytes 12615680 | tf_op jit(solution)/shard_map/convert_element_type | solution.py:269
  209.6 8.9 %all-to-all-done.3 = bf16[16,64,768]{2,1,0:T(8,128)(2,1)} async-done(((bf16[16,64,768]{2,1,0:T(8,128)(2,1)}), bf16[16,64,768]{2,1,0:T(8,128)(2,1)}, u32[]{:S(2)}, u32[]{:S(2)}) %all-to-all-start.3) | async-done | bytes 1572896 | tf_op jit(solution)/shard_map/all_to_all | solution.py:212
  218.6 1.5 slice_bitcast_fusion
  220.1 1.1 slice_bitcast_fusion.1
  222.1 4.9 %psum.7 = bf16[1,256,64]{1,2,0:T(8,128)(2,1)S(1)} all-reduce(f32[1,256,64]{1,2,0:T(8,128)S(1)} %convolution_bitcast_fusion), channel_id=1, replica_groups=mesh['req'=16,'head'=2] {'head'}, use_global_device_ids=true, to_apply=%region_4.5 | all-reduce | flops 16384 | bytes 98304 | tf_op jit(solution)/shard_map/psum | solution.py:273
  227.0 2.0 fusion.9
  (108 shorter events, 14.0 us)
Async XLA Ops:
  0.6 100.2 %copy-start = (s32[16]{0:T(128)S(1)}, s32[16]{0:T(128)}, u32[]{:S(2)}) copy-start(s32[16]{0:T(128)} %param.28) | copy-start | bytes 196
  26.6 9.1 %copy-start.30 = (f32[128]{0:T(128)S(1)}, f32[128]{0:T(128)}, u32[]{:S(2)}) copy-start(f32[128]{0:T(128)} %param.24) | copy-start | bytes 1540
  26.6 9.1 %copy-start.29 = (f32[128]{0:T(128)S(1)}, f32[128]{0:T(128)}, u32[]{:S(2)}) copy-start(f32[128]{0:T(128)} %param.25) | copy-start | bytes 1540
  26.7 9.2 %copy-start.23 = (f32[4,4,2,128]{3,2,1,0:T(2,128)S(1)}, f32[4,4,2,128]{3,2,1,0:T(2,128)}, u32[]{:S(2)}) copy-start(f32[4,4,2,128]{3,2,1,0:T(2,128)} %param.22) | copy-start | bytes 49156
  26.7 11.6 %copy-start.12 = (f32[8192]{0:T(1024)S(1)}, f32[8192]{0:T(1024)}, u32[]{:S(2)}) copy-start(f32[8192]{0:T(1024)} %param.26) | copy-start | bytes 98308
  26.7 12.2 %copy-start.18 = (bf16[16,16,128]{2,1,0:T(8,128)(2,1)S(1)}, bf16[16,16,128]{2,1,0:T(8,128)(2,1)}, u32[]{:S(2)}) copy-start(bf16[16,16,128]{2,1,0:T(8,128)(2,1)} %get-tuple-element.7) | copy-start | bytes 196612
  26.7 12.9 %copy-start.10 = (bf16[256,128]{1,0:T(8,128)(2,1)S(1)}, bf16[256,128]{1,0:T(8,128)(2,1)}, u32[]{:S(2)}) copy-start(bf16[256,128]{1,0:T(8,128)(2,1)} %param.20) | copy-start | bytes 196612
  26.7 12.9 %copy-start.24 = (f32[128]{0:T(128)S(1)}, f32[128]{0:T(128)}, u32[]{:S(2)}) copy-start(f32[128]{0:T(128)} %param.23) | copy-start | bytes 1540
  26.7 14.0 %copy-start.7 = (bf16[1,64,4096]{2,1,0:T(8,128)(2,1)S(1)}, bf16[1,64,4096]{2,1,0:T(8,128)(2,1)}, u32[]{:S(2)}) copy-start(bf16[1,64,4096]{2,1,0:T(8,128)(2,1)} %param.32) | copy-start | bytes 1572868
  29.9 54.0 %all-to-all-start.1 = ((bf16[16,512,128]{2,1,0:T(8,128)(2,1)}), bf16[16,512,128]{2,1,0:T(8,128)(2,1)S(1)}, u32[]{:S(2)}, u32[]{:S(2)}) async-start(bf16[16,512,128]{2,1,0:T(8,128)(2,1)} %bitcast.147), calls=%async_computation.1 | async-start | bytes 4194304 | tf_op jit(solution)/shard_map/all_to_all | solution.py:207
  40.8 3.7 %copy-start.11 = (bf16[256,128]{1,0:T(8,128)(2,1)S(1)}, bf16[256,128]{1,0:T(8,128)(2,1)}, u32[]{:S(2)}) copy-start(bf16[256,128]{1,0:T(8,128)(2,1)} %param.20) | copy-start | bytes 196612
  40.8 3.7 %copy-start.25 = (f32[128]{0:T(128)S(1)}, f32[128]{0:T(128)}, u32[]{:S(2)}) copy-start(f32[128]{0:T(128)} %param.23) | copy-start | bytes 1540
  43.2 48.5 %copy-start.5 = (bf16[256,4,2,128]{3,2,1,0:T(2,128)(2,1)S(1)}, bf16[256,4,2,128]{3,2,1,0:T(2,128)(2,1)}, u32[]{:S(2)}) copy-start(bf16[256,4,2,128]{3,2,1,0:T(2,128)(2,1)} %param.19) | copy-start | bytes 1572868
  83.9 41.4 %all-to-all-start = ((bf16[16,64,768]{2,1,0:T(8,128)(2,1)}), bf16[16,64,768]{2,1,0:T(8,128)(2,1)}, u32[]{:S(2)}, u32[]{:S(2)}) async-start(bf16[16,64,768]{2,1,0:T(8,128)(2,1)} %pad_maximum_fusion.1), calls=%async_computation | async-start | bytes 3145728 | tf_op jit(solution)/shard_map/all_to_all | solution.py:200
  94.4 6.4 %copy-start.28 = (s32[16]{0:T(128)S(1)}, s32[16]{0:T(128)}, u32[]{:S(2)}) copy-start(s32[16]{0:T(128)} %get-tuple-element.13) | copy-start | bytes 196
  94.4 7.1 %copy-start.27 = (s32[16]{0:T(128)S(1)}, s32[16]{0:T(128)}, u32[]{:S(2)}) copy-start(s32[16]{0:T(128)} %get-tuple-element.11) | copy-start | bytes 196
  94.4 7.2 %copy-start.19 = (f32[4,2,128]{2,0,1:T(4,128)S(1)}, f32[4,2,128]{2,0,1:T(4,128)}, u32[]{:S(2)}) copy-start(f32[4,2,128]{2,0,1:T(4,128)} %copy.58) | copy-start | bytes 12292
  94.4 7.2 %copy-start.20 = (f32[4,2,128]{2,0,1:T(4,128)S(1)}, f32[4,2,128]{2,0,1:T(4,128)}, u32[]{:S(2)}) copy-start(f32[4,2,128]{2,0,1:T(4,128)} %copy.61) | copy-start | bytes 12292
  94.4 7.2 %copy-start.21 = (f32[4,2,128]{2,0,1:T(4,128)S(1)}, f32[4,2,128]{2,0,1:T(4,128)}, u32[]{:S(2)}) copy-start(f32[4,2,128]{2,0,1:T(4,128)} %copy.63) | copy-start | bytes 12292
  94.4 7.2 %copy-start.22 = (f32[4,2,128]{2,0,1:T(4,128)S(1)}, f32[4,2,128]{2,0,1:T(4,128)}, u32[]{:S(2)}) copy-start(f32[4,2,128]{2,0,1:T(4,128)} %copy.62) | copy-start | bytes 12292
  94.4 10.9 %copy-start.14 = (f32[4,8192]{1,0:T(4,128)S(1)}, f32[4,8192]{1,0:T(4,128)}, u32[]{:S(2)}) copy-start(f32[4,8192]{1,0:T(4,128)} %param.21) | copy-start | bytes 393220
  125.3 51.8 %all-to-all-start.2 = ((bf16[16,512,128]{2,1,0:T(8,128)(2,1)}), bf16[16,512,128]{2,1,0:T(8,128)(2,1)S(1)}, u32[]{:S(2)}, u32[]{:S(2)}) async-start(bf16[16,512,128]{2,1,0:T(8,128)(2,1)} %gather_fusion.2), calls=%async_computation.2 | async-start | bytes 4194304 | tf_op jit(solution)/shard_map/all_to_all | solution.py:209
  129.0 16.9 %copy-start.6 = (f32[4,256,256]{2,1,0:T(8,128)S(1)}, f32[4,256,256]{2,1,0:T(8,128)}, u32[]{:S(2)}) copy-start(f32[4,256,256]{2,1,0:T(8,128)} %fusion.20) | copy-start | bytes 3145732
  129.0 16.9 %copy-start.15 = (f32[1,256,128]{1,2,0:T(8,128)S(1)}, f32[1,256,128]{1,2,0:T(8,128)}, u32[]{:S(2)}) copy-start(f32[1,256,128]{1,2,0:T(8,128)} %copy.67) | copy-start | bytes 393220
  129.0 16.9 %copy-start.17 = (f32[256,128]{0,1:T(8,128)S(1)}, f32[256,128]{0,1:T(8,128)}, u32[]{:S(2)}) copy-start(f32[256,128]{0,1:T(8,128)} %copy.68) | copy-start | bytes 393220
  177.1 41.4 %all-to-all-start.3 = ((bf16[16,64,768]{2,1,0:T(8,128)(2,1)}), bf16[16,64,768]{2,1,0:T(8,128)(2,1)}, u32[]{:S(2)}, u32[]{:S(2)}) async-start(bf16[16,64,768]{2,1,0:T(8,128)(2,1)} %gather_fusion.1), calls=%async_computation.3 | async-start | bytes 3145728 | tf_op jit(solution)/shard_map/all_to_all | solution.py:212
  181.6 5.9 %copy-start.9 = (f32[4,32,64]{2,1,0:T(8,128)S(1)}, f32[4,32,64]{2,1,0:T(8,128)}, u32[]{:S(2)}) copy-start(f32[4,32,64]{2,1,0:T(8,128)} %mul.263) | copy-start | bytes 98308
  192.8 9.0 %copy-start.16 = (f32[1,256,128]{1,2,0:T(8,128)S(1)}, f32[1,256,128]{1,2,0:T(8,128)}, u32[]{:S(2)}) copy-start(f32[1,256,128]{1,2,0:T(8,128)} %copy.75) | copy-start | bytes 393220
  192.8 9.0 %copy-start.26 = (f32[4,32]{1,0:T(4,128)S(1)}, f32[4,32]{1,0:T(4,128)}, u32[]{:S(2)}) copy-start(f32[4,32]{1,0:T(4,128)} %exp.53) | copy-start | bytes 1540
  201.8 5.1 %copy-start.2 = (f32[256,8192]{1,0:T(8,128)S(1)}, f32[256,8192]{1,0:T(8,128)}, u32[]{:S(2)}) copy-start(f32[256,8192]{1,0:T(8,128)} %copy.72) | copy-start | bytes 25165828
  201.8 5.1 %copy-start.13 = (f32[8192]{0:T(1024)S(1)}, f32[8192]{0:T(1024)}, u32[]{:S(2)}) copy-start(f32[8192]{0:T(1024)} %param.26) | copy-start | bytes 98308
  221.2 7.8 %copy-start.1 = (s32[16]{0:T(128)S(1)}, s32[16]{0:T(128)}, u32[]{:S(2)}) copy-start(s32[16]{0:T(128)} %param.28) | copy-start | bytes 196
  (3 other events, 5.4 us)

commit v3 on v2

--- a/solution.py
+++ b/solution.py
@@ -204,6 +204,7 @@
     my_slot = jnp.sum(jnp.where(owner_all == me, slot_all, 0))
     my_state = lax.dynamic_index_in_dim(cached_ssm_states, my_slot, 0, keepdims=False)
     state_pieces = my_state.reshape(n, heads_dev * head_size // n, state_size)
+    state_pieces, panels = lax.optimization_barrier((state_pieces, panels))
     state_pieces = lax.all_to_all(state_pieces, "req", split_axis=0, concat_axis=0, tiled=True)
     state_pieces = jnp.take(state_pieces, owner_all, axis=0, mode="clip")
     state_pieces = lax.all_to_all(state_pieces, "req", split_axis=0, concat_axis=0, tiled=True)

time: 230 us -> 230 us (level)
  waiting for transfers between devices: 83 us -> 56.2 us
  Pallas kernels: 16.6 us -> 42.8 us
  starting transfers between devices: 18.3 us -> 21.4 us
    pallas_call x1, Pallas kernels: 16.6 us -> 42.8 us  [exchange(): pl.pallas_call(functools.partial(exchange_kernel, n), out_shape=(jax.Shap...]
    all_to_all x2, waiting for transfers between devices: 26.6 us -> 9.04 us  [per_device(): lax.all_to_all(panels, 'req', split_axis=0, concat_axis=0, tiled=True)]
    all_to_all x2, waiting for transfers between devices: 56.4 us -> 47.2 us  [per_device(): lax.all_to_all(state_pieces, 'req', split_axis=0, concat_axis=0, tiled=True)]
    all_to_all x2, starting transfers between devices: 8.79 us -> 11.2 us  [per_device(): lax.all_to_all(panels, 'req', split_axis=0, concat_axis=0, tiled=True)]
    unnamed x69 -> x47, local copies, waits for them, and re-layouts: 14.3 us -> 15.8 us
  transfers between devices with their start and end apart: 4 -> 4, of which waited for: 4 -> 3; matrix products, arithmetic and copies ran while one was open for 37% -> 36% of each run, Pallas kernels for 0% -> 19%
where the time goes in v3:
time: 230 us; the launch traced here: 229 us
  waiting for transfers between devices  56.2 us (24%)
  local copies, waits for them, and re-layouts  43 us (19%)
  Pallas kernels  42.8 us (19%)
  other arithmetic  30.2 us (13%)
  matrix products  25.9 us (11%)
  starting transfers between devices  21.4 us (9%)
  between operations  4.93 us (2%)
  blocking collectives  4.92 us (2%)
    all_to_all x2, waiting for transfers between devices, per_device(): lax.all_to_all(state_pieces, 'req', split_axis=0, concat_axis=0, tiled=True)  47.2 us
    pallas_call x1, Pallas kernels, exchange(): pl.pallas_call(functools.partial(exchange_kernel, n), out_shape=(jax.Shap...  42.8 us
    convert_element_type x2, other arithmetic, causal_conv(): return jax.nn.silu(summed).astype(jnp.bfloat16)  17.3 us
    unnamed x47, local copies, waits for them, and re-layouts  15.8 us
    all_to_all x2, starting transfers between devices, per_device(): lax.all_to_all(panels, 'req', split_axis=0, concat_axis=0, tiled=True)  11.2 us
    dot_general x1, matrix products, per_device(): jnp.einsum('rghts,rsghp->rtghp', mix_weights, conv_heads, preferred_eleme...  10.8 us
    all_to_all x2, starting transfers between devices, per_device(): lax.all_to_all(state_pieces, 'req', split_axis=0, concat_axis=0, tiled=True)  10.2 us
    all_to_all x2, waiting for transfers between devices, per_device(): lax.all_to_all(panels, 'req', split_axis=0, concat_axis=0, tiled=True)  9.04 us
  transfers between devices with their start and end apart: 4, of which 3 were waited for; matrix products, arithmetic and copies ran while one was open for 36% of the time, Pallas kernels for 19%

profile of v3, /device:TPU:13, one launch (start us, length us, event | category | flops | bytes accessed | tf_op | source)
XLA Modules:
  0.0 229.2 jit_solution(8612442676131463889)
XLA Ops:
  0.6 1.1 copy.82
  2.0 1.6 copy.81
  4.2 1.3 pad_maximum_fusion.1
  5.5 6.7 %all-to-all-start = ((bf16[16,64,768]{2,1,0:T(8,128)(2,1)}), bf16[16,64,768]{2,1,0:T(8,128)(2,1)S(1)}, u32[]{:S(2)}, u32[]{:S(2)}) async-start(bf16[16,64,768]{2,1,0:T(8,128)(2,1)} %pad_maximum_fusion.1), calls=%async_computation | async-start | bytes 3145728 | tf_op jit(solution)/shard_map/all_to_all | solution.py:200
  15.9 42.8 %shard_map.193 = (s32[16,8,128]{2,1,0:T(8,128)}, bf16[16,16,128]{2,1,0:T(8,128)(2,1)}) custom-call(s32[8,128]{1,0:T(8,128)} %broadcast_in_dim.38.numbers_ref, bf16[16,2,16,128]{3,2,1,0:T(8,128)(2,1)} %bitcast.160), custom_call_target="tpu_custom_call" | custom-call | bytes 30000000 | tf_op jit(solution)/shard_map/pallas_call | solution.py:123
  58.7 2.3 %slice_reduce_fusion.3 = (s32[16]{0:T(128)S(1)}, s32[16]{0:T(128)S(1)}, s32[]{:T(128)}) fusion(s32[16,8,128]{2,1,0:T(8,128)} %get-tuple-element.10, s32[]{:T(128)S(6)} %axis_index.15), kind=kLoop, calls=%fused_computation.77 | loop fusion | flops 47 | bytes 328 | tf_op jit(solution)/shard_map/slice | solution.py:202
  64.2 3.1 %constant_dynamic-slice_fusion = bf16[1,128,64,128]{3,2,1,0:T(8,128)(2,1)} fusion(bf16[2,128,64,128]{3,2,1,0:T(8,128)(2,1)} %param.33, s32[]{:T(128)S(6)} %select_n.23), kind=kLoop, calls=%fused_computation.91 | loop fusion | bytes 4194308 | tf_op jit(solution)/shard_map/jit(dynamic_index_in_dim)/dynamic_slice | solution.py:205
  67.4 1.2 copy-done.5
  68.6 6.2 %all-to-all-start.1 = ((bf16[16,512,128]{2,1,0:T(8,128)(2,1)}), bf16[16,512,128]{2,1,0:T(8,128)(2,1)S(1)}, u32[]{:S(2)}, u32[]{:S(2)}) async-start(bf16[16,512,128]{2,1,0:T(8,128)(2,1)} %bitcast.35), calls=%async_computation.1 | async-start | bytes 4194304 | tf_op jit(solution)/shard_map/all_to_all | solution.py:208
  78.5 1.8 copy.56
  80.3 6.4 %copy.55 = bf16[256,8192]{0,1:T(8,128)(2,1)} copy(bf16[256,8192]{1,0:T(8,128)(2,1)} %param.18) | data formatting | bytes 8388608 | tf_op args[0]
  88.0 2.5 %multiply_convert_fusion.9 = bf16[1,256,4,2,128]{4,1,2,3,0:T(8,128)(2,1)S(1)} fusion(bf16[1,3,4,2,128]{4,1,2,3,0:T(4,128)(2,1)S(1)} %copy.60, bf16[1,256,4,2,128]{4,1,2,3,0:T(8,128)(2,1)} %bitcast.150, f32[4,2,128]{2,0,1:T(4,128)S(1)} %copy.63, f32[4,2,128]{2,0,1:T(4,128)S(1)} %copy.62, f32[4,2,128]{2,0,1:T(4,128)S(1)} %copy.61, f32[4,2,128]{2,0,1:T(4,128)S(1)} %copy.58, ...), kind=kLoop, calls=%fused_computation.39 | loop fusion | flops 6553600 | bytes 1595392 | tf_op jit(solution)/shard_map/convert_element_type | solution.py:20
  90.5 1.3 fusion.20
  91.8 1.3 fusion.35
  93.0 30.0 %all-to-all-done.1 = bf16[16,512,128]{2,1,0:T(8,128)(2,1)S(1)} async-done(((bf16[16,512,128]{2,1,0:T(8,128)(2,1)}), bf16[16,512,128]{2,1,0:T(8,128)(2,1)S(1)}, u32[]{:S(2)}, u32[]{:S(2)}) %all-to-all-start.1) | async-done | bytes 2097184 | tf_op jit(solution)/shard_map/all_to_all | solution.py:208
  123.0 2.1 gather_fusion.2
  125.1 4.0 %all-to-all-start.2 = ((bf16[16,512,128]{2,1,0:T(8,128)(2,1)}), bf16[16,512,128]{2,1,0:T(8,128)(2,1)S(1)}, u32[]{:S(2)}, u32[]{:S(2)}) async-start(bf16[16,512,128]{2,1,0:T(8,128)(2,1)} %gather_fusion.2), calls=%async_computation.2 | async-start | bytes 4194304 | tf_op jit(solution)/shard_map/all_to_all | solution.py:210
  129.2 14.8 %multiply_convert_fusion.5 = bf16[1,256,8192]{1,2,0:T(8,128)(2,1)S(1)} fusion(bf16[256,8192]{0,1:T(8,128)(2,1)} %copy.55, bf16[1,256,8192]{1,2,0:T(8,128)(2,1)} %bitcast.139, bf16[1,3,8192]{1,2,0:T(8,128)(2,1)} %copy.56, f32[8192]{0:T(1024)S(1)} %bitcast.164, f32[8192]{0:T(1024)S(1)} %bitcast.165, f32[8192]{0:T(1024)S(1)} %bitcast.163, f32[8192]{0:T(1024)S(1)} %bitcast.162), kind=kLoop, calls=%fused_computation.20 | loop fusion | flops 52428800 | bytes 12763136 | tf_op jit(solution)/shard_map/convert_element_type | solution.py:20
  144.0 2.0 copy-done.3
  146.0 10.8 %fusion = f32[4,32,64,256]{3,2,1,0:T(8,128)} fusion(bf16[256,4,32,64]{0,3,2,1:T(8,128)(2,1)S(1)} %bitcast.141, f32[4,32,256]{2,1,0:T(8,128)S(1)} %bitcast.168, f32[4,32,256]{2,1,0:T(8,128)S(1)} %bitcast.167, f32[4,256,256]{2,1,0:T(8,128)S(1)} %copy-done.7, pred[256,256]{1,0:T(8,128)(4,1)S(1)} %copy-done.14), kind=kOutput, calls=%fused_computation.4 | convolution fusion | flops 1115684864 | bytes 13959168 | tf_op jit(solution)/shard_map/rghts,rsghp->rtghp/dot_general | solution.py:255
  156.9 3.2 %gather_fusion.1 = bf16[16,64,768]{2,1,0:T(8,128)(2,1)} fusion(bf16[16,64,768]{2,1,0:T(8,128)(2,1)} %copy-done.5, s32[1024]{0:T(1024)S(1)} %pad_clamp_fusion.1), kind=kCustom, calls=%fused_computation.1 | custom fusion | bytes 3145792 | tf_op jit(solution)/shard_map/jit(_take)/gather | solution.py:211
  160.1 17.2 %all-to-all-done.2 = bf16[16,512,128]{2,1,0:T(8,128)(2,1)S(1)} async-done(((bf16[16,512,128]{2,1,0:T(8,128)(2,1)}), bf16[16,512,128]{2,1,0:T(8,128)(2,1)S(1)}, u32[]{:S(2)}, u32[]{:S(2)}) %all-to-all-start.2) | async-done | bytes 2097184 | tf_op jit(solution)/shard_map/all_to_all | solution.py:210
  177.3 4.5 %all-to-all-start.3 = ((bf16[16,64,768]{2,1,0:T(8,128)(2,1)}), bf16[16,64,768]{2,1,0:T(8,128)(2,1)}, u32[]{:S(2)}, u32[]{:S(2)}) async-start(bf16[16,64,768]{2,1,0:T(8,128)(2,1)} %gather_fusion.1), calls=%async_computation.3 | async-start | bytes 3145728 | tf_op jit(solution)/shard_map/all_to_all | solution.py:213
  181.8 5.8 %multiply_reduce_fusion = (f32[256,4]{0,1:T(4,128)S(1)}, f32[1,256,4,32,64]{1,4,3,2,0:T(8,128)S(1)}) fusion(bf16[1,256,4,32,64]{1,4,3,2,0:T(8,128)(2,1)} %bitcast.142, f32[4,32]{1,0:T(4,128)S(1)} %mul.255, f32[256,4,32]{0,2,1:T(8,128)S(1)} %bitcast.157, bf16[4,32,64,128]{3,2,1,0:T(8,128)(2,1)S(1)} %bitcast.145, ...), kind=kOutput, calls=%fused_computation.19 | convolution fusion | flops 551549952 | bytes 23468032 | tf_op jit(solution)/shard_map/rtgn,rghpn->rtghp/dot_general | solution.py:259
  187.6 5.3 %multiply_convert_fusion.3 = (bf16[1,256,4,32,64]{1,4,3,2,0:T(8,128)(2,1)}, f32[1,256,4,32,64]{1,4,3,2,0:T(8,128)}) fusion(f32[4,32,64]{2,1,0:T(8,128)S(1)} %mul.263, f32[1,256,4,32,64]{1,4,3,2,0:T(8,128)S(1)} %get-tuple-element.35, f32[256,4]{0,1:T(4,128)S(1)} %add_rsqrt_fusion), kind=kLoop, calls=%fused_computation.17 | loop fusion | flops 6291456 | bytes 21008384 | tf_op jit(solution)/shard_map/convert_element_type | solution.py:270
  192.9 8.9 %copy.72 = f32[256,8192]{1,0:T(8,128)} copy(f32[256,8192]{0,1:T(8,128)} %bitcast.140) | data formatting | bytes 16777216 | tf_op jit(solution)/shard_map/reshape | solution.py:266
  201.9 5.1 %add_convert_fusion = bf16[4,32,64,128]{3,2,1,0:T(8,128)(2,1)} fusion(bf16[4,32,64,128]{3,2,1,0:T(8,128)(2,1)S(1)} %bitcast.146, f32[4,32]{1,0:T(4,128)S(1)} %exp.53, bf16[256,4,32,64]{0,3,2,1:T(8,128)(2,1)} %bitcast.143, f32[256,4,32]{0,2,1:T(8,128)S(1)} %bitcast.166, bf16[1,256,4,2,128]{4,1,2,3,0:T(8,128)(2,1)S(1)} %multiply_convert_fusion.9), kind=kOutput, calls=%fused_computation.31 | convolution fusion | flops 547356672 | bytes 8783872 | tf_op jit(solution)/shard_map/rsghp,rsgn->rghpn/dot_general | solution.py:284
  206.9 2.8 %multiply_convert_fusion.4 = bf16[256,8192]{1,0:T(8,128)(2,1)} fusion(f32[256,8192]{1,0:T(8,128)S(1)} %copy-done.2, f32[8192]{0:T(1024)S(1)} %copy-done.9), kind=kLoop, calls=%fused_computation.18 | loop fusion | flops 4194304 | bytes 12615680 | tf_op jit(solution)/shard_map/convert_element_type | solution.py:270
  209.7 9.0 %all-to-all-done.3 = bf16[16,64,768]{2,1,0:T(8,128)(2,1)} async-done(((bf16[16,64,768]{2,1,0:T(8,128)(2,1)}), bf16[16,64,768]{2,1,0:T(8,128)(2,1)}, u32[]{:S(2)}, u32[]{:S(2)}) %all-to-all-start.3) | async-done | bytes 1572896 | tf_op jit(solution)/shard_map/all_to_all | solution.py:213
  218.7 1.5 slice_bitcast_fusion
  222.3 4.9 %psum.7 = bf16[1,256,64]{1,2,0:T(8,128)(2,1)S(1)} all-reduce(f32[1,256,64]{1,2,0:T(8,128)S(1)} %convolution_bitcast_fusion), channel_id=1, replica_groups=mesh['req'=16,'head'=2] {'head'}, use_global_device_ids=true, to_apply=%region_4.5 | all-reduce | flops 16384 | bytes 98304 | tf_op jit(solution)/shard_map/psum | solution.py:274
  227.2 2.0 fusion.9
  (86 shorter events, 10.8 us)
Async XLA Ops:
  0.6 86.0 %copy-start = (s32[16]{0:T(128)S(1)}, s32[16]{0:T(128)}, u32[]{:S(2)}) copy-start(s32[16]{0:T(128)} %param.28) | copy-start | bytes 196
  3.6 10.6 %copy-start.19 = (f32[128]{0:T(128)S(1)}, f32[128]{0:T(128)}, u32[]{:S(2)}) copy-start(f32[128]{0:T(128)} %param.24) | copy-start | bytes 1540
  3.6 10.6 %copy-start.18 = (f32[128]{0:T(128)S(1)}, f32[128]{0:T(128)}, u32[]{:S(2)}) copy-start(f32[128]{0:T(128)} %param.25) | copy-start | bytes 1540
  3.6 10.7 %copy-start.16 = (bf16[2,3,4,2,128]{4,3,2,1,0:T(2,128)(2,1)S(1)}, bf16[2,3,4,2,128]{4,3,2,1,0:T(2,128)(2,1)}, u32[]{:S(2)}) copy-start(bf16[2,3,4,2,128]{4,3,2,1,0:T(2,128)(2,1)} %param.35) | copy-start | bytes 36868
  3.6 10.7 %copy-start.15 = (f32[4,4,2,128]{3,2,1,0:T(2,128)S(1)}, f32[4,4,2,128]{3,2,1,0:T(2,128)}, u32[]{:S(2)}) copy-start(f32[4,4,2,128]{3,2,1,0:T(2,128)} %param.22) | copy-start | bytes 49156
  3.6 10.8 %copy-start.9 = (f32[8192]{0:T(1024)S(1)}, f32[8192]{0:T(1024)}, u32[]{:S(2)}) copy-start(f32[8192]{0:T(1024)} %param.26) | copy-start | bytes 98308
  3.6 10.8 %copy-start.13 = (bf16[2,3,8192]{2,0,1:T(2,128)(2,1)S(1)}, bf16[2,3,8192]{2,0,1:T(2,128)(2,1)}, u32[]{:S(2)}) copy-start(bf16[2,3,8192]{2,0,1:T(2,128)(2,1)} %param.34) | copy-start | bytes 294916
  5.5 61.8 %copy-start.8 = (bf16[256,128]{1,0:T(8,128)(2,1)S(1)}, bf16[256,128]{1,0:T(8,128)(2,1)}, u32[]{:S(2)}) copy-start(bf16[256,128]{1,0:T(8,128)(2,1)} %param.20) | copy-start | bytes 196612
  5.5 61.8 %copy-start.17 = (f32[128]{0:T(128)S(1)}, f32[128]{0:T(128)}, u32[]{:S(2)}) copy-start(f32[128]{0:T(128)} %param.23) | copy-start | bytes 1540
  5.5 61.9 %all-to-all-start = ((bf16[16,64,768]{2,1,0:T(8,128)(2,1)}), bf16[16,64,768]{2,1,0:T(8,128)(2,1)S(1)}, u32[]{:S(2)}, u32[]{:S(2)}) async-start(bf16[16,64,768]{2,1,0:T(8,128)(2,1)} %pad_maximum_fusion.1), calls=%async_computation | async-start | bytes 3145728 | tf_op jit(solution)/shard_map/all_to_all | solution.py:200
  67.3 10.3 %copy-start.6 = (bf16[256,4,2,128]{3,2,1,0:T(2,128)(2,1)S(1)}, bf16[256,4,2,128]{3,2,1,0:T(2,128)(2,1)}, u32[]{:S(2)}) copy-start(bf16[256,4,2,128]{3,2,1,0:T(2,128)(2,1)} %param.19) | copy-start | bytes 1572868
  67.4 1.2 copy-start.5
  68.6 54.4 %all-to-all-start.1 = ((bf16[16,512,128]{2,1,0:T(8,128)(2,1)}), bf16[16,512,128]{2,1,0:T(8,128)(2,1)S(1)}, u32[]{:S(2)}, u32[]{:S(2)}) async-start(bf16[16,512,128]{2,1,0:T(8,128)(2,1)} %bitcast.35), calls=%async_computation.1 | async-start | bytes 4194304 | tf_op jit(solution)/shard_map/all_to_all | solution.py:208
  125.1 52.2 %all-to-all-start.2 = ((bf16[16,512,128]{2,1,0:T(8,128)(2,1)}), bf16[16,512,128]{2,1,0:T(8,128)(2,1)S(1)}, u32[]{:S(2)}, u32[]{:S(2)}) async-start(bf16[16,512,128]{2,1,0:T(8,128)(2,1)} %gather_fusion.2), calls=%async_computation.2 | async-start | bytes 4194304 | tf_op jit(solution)/shard_map/all_to_all | solution.py:210
  129.2 16.9 %copy-start.7 = (f32[4,256,256]{2,1,0:T(8,128)S(1)}, f32[4,256,256]{2,1,0:T(8,128)}, u32[]{:S(2)}) copy-start(f32[4,256,256]{2,1,0:T(8,128)} %fusion.20) | copy-start | bytes 3145732
  129.2 16.9 %copy-start.11 = (f32[1,256,128]{1,2,0:T(8,128)S(1)}, f32[1,256,128]{1,2,0:T(8,128)}, u32[]{:S(2)}) copy-start(f32[1,256,128]{1,2,0:T(8,128)} %copy.67) | copy-start | bytes 393220
  129.2 16.9 %copy-start.12 = (f32[256,128]{0,1:T(8,128)S(1)}, f32[256,128]{0,1:T(8,128)}, u32[]{:S(2)}) copy-start(f32[256,128]{0,1:T(8,128)} %copy.68) | copy-start | bytes 393220
  129.2 16.9 %copy-start.14 = (pred[256,256]{1,0:T(8,128)(4,1)S(1)}, pred[256,256]{1,0:T(8,128)(4,1)}, u32[]{:S(2)}) copy-start(pred[256,256]{1,0:T(8,128)(4,1)} %iota_compare_fusion.1) | copy-start | bytes 196612
  144.0 2.0 copy-start.3
  177.3 41.4 %all-to-all-start.3 = ((bf16[16,64,768]{2,1,0:T(8,128)(2,1)}), bf16[16,64,768]{2,1,0:T(8,128)(2,1)}, u32[]{:S(2)}, u32[]{:S(2)}) async-start(bf16[16,64,768]{2,1,0:T(8,128)(2,1)} %gather_fusion.1), calls=%async_computation.3 | async-start | bytes 3145728 | tf_op jit(solution)/shard_map/all_to_all | solution.py:213
  192.9 8.9 %copy-start.10 = (f32[1,256,128]{1,2,0:T(8,128)S(1)}, f32[1,256,128]{1,2,0:T(8,128)}, u32[]{:S(2)}) copy-start(f32[1,256,128]{1,2,0:T(8,128)} %copy.75) | copy-start | bytes 393220
  201.9 5.1 %copy-start.2 = (f32[256,8192]{1,0:T(8,128)S(1)}, f32[256,8192]{1,0:T(8,128)}, u32[]{:S(2)}) copy-start(f32[256,8192]{1,0:T(8,128)} %copy.72) | copy-start | bytes 25165828
  218.7 2.7 %copy-start.4 = (bf16[1,256,4,32,64]{1,4,3,2,0:T(8,128)(2,1)S(1)}, bf16[1,256,4,32,64]{1,4,3,2,0:T(8,128)(2,1)}, u32[]{:S(2)}) copy-start(bf16[1,256,4,32,64]{1,4,3,2,0:T(8,128)(2,1)} %get-tuple-element.18) | copy-start | bytes 12582916
  221.4 7.9 %copy-start.1 = (s32[16]{0:T(128)S(1)}, s32[16]{0:T(128)}, u32[]{:S(2)}) copy-start(s32[16]{0:T(128)} %param.28) | copy-start | bytes 196
